TPU v7x, 512 devices: a whole 4x4x16 slice. The times are simulated.
512 devices in a mesh: inl: 16 (over z_hi, y, core), xl: 8 (over z_lo), gz: 4 (over x).
Axes of the slice: x: 4, y: 4, z: 16 (z_hi: 2, z_lo: 8; z = z_hi * 8 + z_lo), core: 2. Of those that a mesh axis runs over, the one named last changes fastest.
Arguments:
- wave_p: float32 [32, 128, 1024], P('gz', 'inl', 'xl'), may hold values from -6 to 6
- wave_p_old: float32 [32, 128, 1024], P('gz', 'inl', 'xl'), may hold values from -6 to 6
- wave_q: float32 [32, 128, 1024], P('gz', 'inl', 'xl'), may hold values from -6 to 6
- wave_q_old: float32 [32, 128, 1024], P('gz', 'inl', 'xl'), may hold values from -6 to 6
- courant_square: float32 [32, 128, 1024], P('gz', 'inl', 'xl'), may hold values from 0.05 to 0.11
- thomsen_epsilon: float32 [32, 128, 1024], P('gz', 'inl', 'xl'), may hold values from 0.1 to 0.35
- thomsen_delta: float32 [32, 128, 1024], P('gz', 'inl', 'xl'), may hold values from 0.02 to 0.2
- tilt_angle: float32 [32, 128, 1024], P('gz', 'inl', 'xl'), may hold values from -3.140625 to 3.140625
- azimuth: float32 [32, 128, 1024], P('gz', 'inl', 'xl'), may hold values from -3.140625 to 3.140625
- shear_ratio: float32 [32, 128, 1024], P('gz', 'inl', 'xl'), may hold values from 0.1 to 0.6
- damping: float32 [32, 128, 1024], P('gz', 'inl', 'xl'), may hold values from 0 to 0.3
- trace_samples: float32 [131072, 256], P(('inl', 'xl', 'gz')), may hold values from -6 to 6
- resample_filter: float32 [2, 256], replicated, may hold values from -0.375 to 0.375
- line_gain: float32 [64], replicated, may hold values from 0.5 to 4
- receiver_inline: int32 [131072], P(('inl', 'xl', 'gz')), may hold values from 0 to 127, as said below
- receiver_crossline: int32 [131072], P(('inl', 'xl', 'gz')), may hold values from 0 to 1023, as said below
- shot_line: int32 [131072], P(('inl', 'xl', 'gz')), may hold values from 0 to 63
Outputs:
- next_p: float32 [32, 128, 1024], P('gz', 'inl', 'xl')
- next_q: float32 [32, 128, 1024], P('gz', 'inl', 'xl')
- prior_p: float32 [32, 128, 1024], P('gz', 'inl', 'xl')
- prior_q: float32 [32, 128, 1024], P('gz', 'inl', 'xl')
Inputs may be any that keep to these rules, and one draw needn't show every extreme that they name: In each aligned block of 256 traces (the traces of one device), at most 4 traces lie in one device column (equal receiver_inline // 8 and receiver_crossline // 128); in every block some column holds exactly 4. `receiver_crossline`: see receiver_inline.
All inputs are finite; a program needn't handle non-finite values.
Results may differ from a plain program's by a relative error of at most 0.000075.
Values sent between devices are 32-bit elements; how exact they have to be, the bound alone decides.
A program may use at most 64 MiB of HBM per device.

v0:
```python
import jax
import jax.numpy as jnp
from jax import lax
from jax.sharding import PartitionSpec as P

second_coef = (-205.0 / 72.0, 8.0 / 5.0, -1.0 / 5.0, 8.0 / 315.0, -1.0 / 560.0)
first_coef = (0.0, 4.0 / 5.0, -1.0 / 5.0, 4.0 / 105.0, -1.0 / 280.0)


def with_halo(block, sides, width):
    for axis, dim in sides:
        count = lax.axis_size(axis)
        forward = [(i, i + 1) for i in range(count - 1)]
        backward = [(target, source) for source, target in forward]
        low = lax.ppermute(
            lax.slice_in_dim(block, block.shape[dim] - width, None, axis=dim), axis, forward
        )
        high = lax.ppermute(lax.slice_in_dim(block, 0, width, axis=dim), axis, backward)
        block = jnp.concatenate([low, block, high], axis=dim)
    return block


def derivatives(padded):
    depth = padded.shape[-3] - 8
    across = padded.shape[-2] - 8
    along = padded.shape[-1] - 8

    def piece(dz, dx, dy):
        return padded[
            ..., 4 + dz : 4 + dz + depth, 4 + dx : 4 + dx + across, 4 + dy : 4 + dy + along
        ]

    center = piece(0, 0, 0)
    u_zz = second_coef[0] * center
    u_xx = second_coef[0] * center
    u_yy = second_coef[0] * center
    for k in range(1, 5):
        u_zz = u_zz + second_coef[k] * (piece(k, 0, 0) + piece(-k, 0, 0))
        u_xx = u_xx + second_coef[k] * (piece(0, k, 0) + piece(0, -k, 0))
        u_yy = u_yy + second_coef[k] * (piece(0, 0, k) + piece(0, 0, -k))
    grad_x = first_coef[1] * (padded[..., :, 5 : 5 + across, :] - padded[..., :, 3 : 3 + across, :])
    grad_y = first_coef[1] * (
        padded[..., :, 4 : 4 + across, 5 : 5 + along]
        - padded[..., :, 4 : 4 + across, 3 : 3 + along]
    )
    for k in range(2, 5):
        grad_x = grad_x + first_coef[k] * (
            padded[..., :, 4 + k : 4 + k + across, :] - padded[..., :, 4 - k : 4 - k + across, :]
        )
        grad_y = grad_y + first_coef[k] * (
            padded[..., :, 4 : 4 + across, 4 + k : 4 + k + along]
            - padded[..., :, 4 : 4 + across, 4 - k : 4 - k + along]
        )
    u_xy = first_coef[1] * (
        grad_x[..., 4 : 4 + depth, :, 5 : 5 + along] - grad_x[..., 4 : 4 + depth, :, 3 : 3 + along]
    )
    u_xz = first_coef[1] * (
        grad_x[..., 5 : 5 + depth, :, 4 : 4 + along] - grad_x[..., 3 : 3 + depth, :, 4 : 4 + along]
    )
    u_yz = first_coef[1] * (grad_y[..., 5 : 5 + depth, :, :] - grad_y[..., 3 : 3 + depth, :, :])
    for k in range(2, 5):
        u_xy = u_xy + first_coef[k] * (
            grad_x[..., 4 : 4 + depth, :, 4 + k : 4 + k + along]
            - grad_x[..., 4 : 4 + depth, :, 4 - k : 4 - k + along]
        )
        u_xz = u_xz + first_coef[k] * (
            grad_x[..., 4 + k : 4 + k + depth, :, 4 : 4 + along]
            - grad_x[..., 4 - k : 4 - k + depth, :, 4 : 4 + along]
        )
        u_yz = u_yz + first_coef[k] * (
            grad_y[..., 4 + k : 4 + k + depth, :, :] - grad_y[..., 4 - k : 4 - k + depth, :, :]
        )
    return (u_zz, u_xx, u_yy, u_xy, u_xz, u_yz)


def anisotropy(tilt_angle, azimuth):
    sin_t = jnp.sin(tilt_angle)
    cos_t = jnp.cos(tilt_angle)
    sin_f = jnp.sin(azimuth)
    cos_f = jnp.cos(azimuth)
    a_xx = sin_t * sin_t * cos_f * cos_f
    a_yy = sin_t * sin_t * sin_f * sin_f
    a_zz = cos_t * cos_t
    a_xy = 2.0 * sin_t * sin_t * sin_f * cos_f
    a_xz = 2.0 * sin_t * cos_t * cos_f
    a_yz = 2.0 * sin_t * cos_t * sin_f
    return (a_xx, a_yy, a_zz, a_xy, a_xz, a_yz)


def advance(padded, current, previous, fields, coefs, plane, top):
    courant, eps_field, delta_field, shear, damp = fields
    a_xx, a_yy, a_zz, a_xy, a_xz, a_yz = coefs
    u_zz, u_xx, u_yy, u_xy, u_xz, u_yz = derivatives(padded)
    h_one = a_xx * u_xx + a_yy * u_yy + a_zz * u_zz + a_xy * u_xy + a_xz * u_xz + a_yz * u_yz
    h_two = u_xx + u_yy + u_zz - h_one
    wave_a = current[0]
    wave_b = current[1]
    old_a = previous[0]
    old_b = previous[1]
    new_a = (
        2.0 * wave_a
        - old_a
        + courant * ((1.0 + 2.0 * eps_field) * h_two[0] + h_one[1] + shear * (h_one[0] - h_one[1]))
        - damp * (wave_a - old_a)
    )
    new_b = (
        2.0 * wave_b
        - old_b
        + courant
        * ((1.0 + 2.0 * delta_field) * h_two[0] + h_one[1] + shear * (h_two[1] - h_two[0]))
        - damp * (wave_b - old_b)
    )
    new_a = new_a.at[top].add(plane)
    new_b = new_b.at[top].add(plane)
    return jnp.stack([new_a, new_b])


def step_amplitudes(samples, resample_filter, line_gain, lines):
    table = jnp.arange(line_gain.shape[0], dtype=jnp.int32)
    gains = jnp.sum(jnp.where(lines[:, None] == table[None, :], line_gain[None, :], 0.0), axis=1)
    return jnp.dot(samples, resample_filter.T, precision=lax.Precision.HIGHEST) * gains[:, None]


def local(
    wave_p,
    wave_p_old,
    wave_q,
    wave_q_old,
    courant_square,
    thomsen_epsilon,
    thomsen_delta,
    tilt_angle,
    azimuth,
    shear_ratio,
    damping,
    trace_samples,
    resample_filter,
    line_gain,
    receiver_inline,
    receiver_crossline,
    shot_line,
):
    depth, inline_cells, cross_cells = wave_p.shape
    cells = inline_cells * cross_cells
    steps = resample_filter.shape[0]
    xl_count = lax.axis_size("xl")
    columns = lax.axis_size("inl") * xl_count
    capacity = 2 * trace_samples.shape[0] // columns
    owner = receiver_inline // inline_cells * xl_count + receiver_crossline // cross_cells
    local_cell = receiver_inline % inline_cells * cross_cells + receiver_crossline % cross_cells
    payload = step_amplitudes(trace_samples, resample_filter, line_gain, shot_line)
    onehot = (owner[:, None] == jnp.arange(columns, dtype=jnp.int32)[None, :]).astype(jnp.int32)
    rank = jnp.sum(jnp.cumsum(onehot, axis=0) * onehot, axis=1) - 1
    slot = owner * capacity + rank
    width = payload.shape[1]
    float_buffer = (
        jnp.zeros((columns * capacity, width), jnp.float32)
        .at[slot]
        .set(payload)
        .reshape(columns, capacity, width)
    )
    label_buffer = (
        jnp.full((columns * capacity,), -1, jnp.int32)
        .at[slot]
        .set(local_cell)
        .reshape(columns, capacity)
    )
    arrived, arrived_labels = (
        lax.all_to_all(float_buffer, ("inl", "xl"), split_axis=0, concat_axis=0, tiled=True),
        lax.all_to_all(label_buffer, ("inl", "xl"), split_axis=0, concat_axis=0, tiled=True),
    )
    amplitude = arrived.reshape(-1, width)
    flat_labels = arrived_labels.reshape(-1)
    target = jnp.where(flat_labels >= 0, flat_labels, cells)
    planes = jnp.zeros((steps, cells), jnp.float32).at[:, target].add(amplitude.T, mode="drop")
    planes = lax.psum(planes, "gz")
    surface_flag = jnp.where(lax.axis_index("gz") == 0, 1.0, 0.0).astype(jnp.float32)
    planes = planes.reshape(steps, inline_cells, cross_cells) * surface_flag
    fields = (courant_square, thomsen_epsilon, thomsen_delta, shear_ratio, damping)
    current = jnp.stack([wave_p, wave_q])
    previous = jnp.stack([wave_p_old, wave_q_old])
    coefs = anisotropy(tilt_angle, azimuth)
    for step in range(steps):
        padded = with_halo(current, (("inl", 2), ("xl", 3), ("gz", 1)), 4)
        newer = advance(padded, current, previous, fields, coefs, planes[step], 0)
        previous = current
        current = newer
    return (current[0], current[1], previous[0], previous[1])


def solution(mesh):
    return jax.shard_map(
        local,
        mesh=mesh,
        in_specs=(
            P("gz", "inl", "xl"),
            P("gz", "inl", "xl"),
            P("gz", "inl", "xl"),
            P("gz", "inl", "xl"),
            P("gz", "inl", "xl"),
            P("gz", "inl", "xl"),
            P("gz", "inl", "xl"),
            P("gz", "inl", "xl"),
            P("gz", "inl", "xl"),
            P("gz", "inl", "xl"),
            P("gz", "inl", "xl"),
            P(("inl", "xl", "gz"), None),
            P(),
            P(),
            P(("inl", "xl", "gz")),
            P(("inl", "xl", "gz")),
            P(("inl", "xl", "gz")),
        ),
        out_specs=(
            P("gz", "inl", "xl"),
            P("gz", "inl", "xl"),
            P("gz", "inl", "xl"),
            P("gz", "inl", "xl"),
        ),
        check_vma=False,
    )
```

profile of v0, /device:TPU:61, one launch (start us, length us, event | category | flops | bytes accessed | tf_op | source)
XLA Modules:
  0.0 165.2 jit_solution(12507482604008025999)
XLA Ops:
  0.6 0.7 fusion.180
  1.5 0.2 fusion.16
  2.0 1.4 scatter_custom_fusion
  3.4 0.7 all_to_all.9
  4.2 19.5 %all-to-all-start = ((s32[128,1,4]{2,1,0:T(1,128)}), s32[128,1,4]{2,1,0:T(1,128)S(1)}, u32[]{:S(2)}, u32[]{:S(2)}) async-start(s32[128,1,4]{2,1,0:T(1,128)} %bitcast.9), calls=%async_computation | async-start | bytes 131072 | tf_op jit(solution)/shard_map/all_to_all | solution.py:170
  23.8 11.2 %collective-permute-start.1 = (f32[2,8,4,128]{3,2,1,0:T(4,128)S(1)}, f32[2,8,4,128]{3,2,1,0:T(4,128)S(1)}, u32[]{:S(2)}, u32[]{:S(2)}) collective-permute-start(f32[2,8,4,128]{3,2,1,0:T(4,128)S(1)} %get-tuple-element.85), channel_id=1, source_target_pairs={{0,32},{32,64},{64,96},{96,128},{128,160},{160,192},{192,224},{224... | collective-permute-start | bytes 98312 | tf_op jit(solution)/shard_map/ppermute | solution.py:15
  35.0 1.9 %collective-permute-start = (f32[2,8,4,128]{3,2,1,0:T(4,128)S(1)}, f32[2,8,4,128]{3,2,1,0:T(4,128)S(1)}, u32[]{:S(2)}, u32[]{:S(2)}) collective-permute-start(f32[2,8,4,128]{3,2,1,0:T(4,128)S(1)} %get-tuple-element.86), channel_id=1, source_target_pairs={{32,0},{64,32},{96,64},{128,96},{160,128},{192,160},{224,192},{256... | collective-permute-start | bytes 98312 | tf_op jit(solution)/shard_map/ppermute | solution.py:18
  37.1 0.2 fusion.189
  37.4 0.6 copy-done.16
  38.0 0.3 convolution_multiply_fusion
  38.5 1.2 scatter_custom_fusion.1
  39.7 1.5 copy.40
  41.2 16.9 %all-to-all-start.1 = ((f32[128,4,2]{1,2,0:T(2,128)}), f32[128,4,2]{1,2,0:T(2,128)S(1)}, u32[]{:S(2)}, u32[]{:S(2)}) async-start(f32[128,4,2]{1,2,0:T(2,128)} %copy.40), calls=%async_computation.1 | async-start | bytes 262144 | tf_op jit(solution)/shard_map/all_to_all | solution.py:169
  58.1 0.5 broadcast.340
  58.6 0.8 reduce.15
  59.6 14.5 %all-to-all-done.1 = f32[128,4,2]{1,2,0:T(2,128)S(1)} async-done(((f32[128,4,2]{1,2,0:T(2,128)}), f32[128,4,2]{1,2,0:T(2,128)S(1)}, u32[]{:S(2)}, u32[]{:S(2)}) %all-to-all-start.1) | async-done | bytes 4128 | tf_op jit(solution)/shard_map/all_to_all | solution.py:169
  74.0 0.9 copy.43
  74.9 2.4 %scatter_custom_fusion.2 = f32[2,1024]{0,1:T(8,128)S(1)} fusion(s32[512]{0:T(512)S(1)} %bitcast.144, f32[512,2]{1,0:T(8,128)S(1)} %bitcast.141, f32[]{:T(128)} %constant.176.clone.1), kind=kCustom, calls=%fused_computation.37 | custom fusion | flops 1024 | bytes 8196 | tf_op jit(solution)/shard_map/scatter-add | solution.py:175
  77.3 17.4 %psum.7 = f32[2,1024]{0,1:T(8,128)S(1)} all-reduce(f32[2,1024]{0,1:T(8,128)S(1)} %scatter_custom_fusion.2), channel_id=1, replica_groups=mesh['inl'=16,'xl'=8,'gz'=4] {'gz'}, use_global_device_ids=true, to_apply=%region_7.8 | all-reduce | flops 2048 | bytes 16384 | tf_op jit(solution)/shard_map/psum | solution.py:176
  94.7 0.5 slice_reduce_fusion
  95.4 3.4 %collective-permute-start.3 = (f32[2,8,16,4]{3,2,1,0:T(8,128)S(1)}, f32[2,8,16,4]{3,2,1,0:T(8,128)S(1)}, u32[]{:S(2)}, u32[]{:S(2)}) collective-permute-start(f32[2,8,16,4]{3,2,1,0:T(8,128)S(1)} %get-tuple-element.72), channel_id=1, source_target_pairs={{0,4},{4,8},{8,12},{12,16},{16,20},{20,24},{24,28},{1,5},{5,9},{9,... | collective-permute-start | bytes 12296 | tf_op jit(solution)/shard_map/ppermute | solution.py:15
  98.8 1.9 %collective-permute-start.2 = (f32[2,8,16,4]{3,2,1,0:T(8,128)S(1)}, f32[2,8,16,4]{3,2,1,0:T(8,128)S(1)}, u32[]{:S(2)}, u32[]{:S(2)}) collective-permute-start(f32[2,8,16,4]{3,2,1,0:T(8,128)S(1)} %get-tuple-element.73), channel_id=1, source_target_pairs={{4,0},{8,4},{12,8},{16,12},{20,16},{24,20},{28,24},{5,1},{9,5},{13... | collective-permute-start | bytes 12296 | tf_op jit(solution)/shard_map/ppermute | solution.py:18
  100.7 0.3 collective-permute-done.3
  101.1 3.7 %collective-permute-done.2 = f32[2,8,16,4]{3,2,1,0:T(8,128)S(1)} collective-permute-done((f32[2,8,16,4]{3,2,1,0:T(8,128)S(1)}, f32[2,8,16,4]{3,2,1,0:T(8,128)S(1)}, u32[]{:S(2)}, u32[]{:S(2)}) %collective-permute-start.2) | collective-permute-done | bytes 4128 | tf_op jit(solution)/shard_map/ppermute | solution.py:18
  104.8 0.2 pad_maximum_fusion.3
  105.0 1.9 %collective-permute-start.4 = (f32[2,4,16,136]{3,2,1,0:T(8,128)S(1)}, f32[2,4,16,136]{3,2,1,0:T(8,128)S(1)}, u32[]{:S(2)}, u32[]{:S(2)}) collective-permute-start(f32[2,4,16,136]{3,2,1,0:T(8,128)S(1)} %get-tuple-element.60), channel_id=1, source_target_pairs={{1,0},{2,1},{3,2},{5,4},{6,5},{7,6},{9,8},{10,9},{11,10},{13,12},{... | collective-permute-start | bytes 208904 | tf_op jit(solution)/shard_map/ppermute | solution.py:18
  107.0 3.5 %collective-permute-start.5 = (f32[2,4,16,136]{3,2,1,0:T(8,128)S(1)}, f32[2,4,16,136]{3,2,1,0:T(8,128)S(1)}, u32[]{:S(2)}, u32[]{:S(2)}) collective-permute-start(f32[2,4,16,136]{3,2,1,0:T(8,128)S(1)} %get-tuple-element.61), channel_id=1, source_target_pairs={{0,1},{1,2},{2,3},{4,5},{5,6},{6,7},{8,9},{9,10},{10,11},{12,13},{... | collective-permute-start | bytes 208904 | tf_op jit(solution)/shard_map/ppermute | solution.py:15
  110.5 0.2 pad_maximum_fusion.2
  110.8 2.5 %collective-permute-done.5 = f32[2,4,16,136]{3,2,1,0:T(8,128)S(1)} collective-permute-done((f32[2,4,16,136]{3,2,1,0:T(8,128)S(1)}, f32[2,4,16,136]{3,2,1,0:T(8,128)S(1)}, u32[]{:S(2)}, u32[]{:S(2)}) %collective-permute-start.5) | collective-permute-done | bytes 69664 | tf_op jit(solution)/shard_map/ppermute | solution.py:15
  113.3 0.2 pad_maximum_fusion
  113.5 0.3 fusion.25
  113.8 0.2 fusion.8
  114.1 0.6 add_subtract_fusion.1
  115.0 10.5 %collective-permute-start.7 = (f32[2,8,4,128]{3,2,1,0:T(4,128)S(1)}, f32[2,8,4,128]{3,2,1,0:T(4,128)S(1)}, u32[]{:S(2)}, u32[]{:S(2)}) collective-permute-start(f32[2,8,4,128]{3,2,1,0:T(4,128)S(1)} %get-tuple-element.76), channel_id=1, source_target_pairs={{0,32},{32,64},{64,96},{96,128},{128,160},{160,192},{192,224},{224... | collective-permute-start | bytes 98312 | tf_op jit(solution)/shard_map/ppermute | solution.py:15
  125.6 1.9 %collective-permute-start.6 = (f32[2,8,4,128]{3,2,1,0:T(4,128)S(1)}, f32[2,8,4,128]{3,2,1,0:T(4,128)S(1)}, u32[]{:S(2)}, u32[]{:S(2)}) collective-permute-start(f32[2,8,4,128]{3,2,1,0:T(4,128)S(1)} %get-tuple-element.77), channel_id=1, source_target_pairs={{32,0},{64,32},{96,64},{128,96},{160,128},{192,160},{224,192},{256... | collective-permute-start | bytes 98312 | tf_op jit(solution)/shard_map/ppermute | solution.py:18
  127.5 14.1 %collective-permute-done.6 = f32[2,8,4,128]{3,2,1,0:T(4,128)S(1)} collective-permute-done((f32[2,8,4,128]{3,2,1,0:T(4,128)S(1)}, f32[2,8,4,128]{3,2,1,0:T(4,128)S(1)}, u32[]{:S(2)}, u32[]{:S(2)}) %collective-permute-start.6) | collective-permute-done | bytes 32800 | tf_op jit(solution)/shard_map/ppermute | solution.py:18
  141.8 3.8 %collective-permute-start.9 = (f32[2,8,16,4]{3,2,1,0:T(8,128)S(1)}, f32[2,8,16,4]{3,2,1,0:T(8,128)S(1)}, u32[]{:S(2)}, u32[]{:S(2)}) collective-permute-start(f32[2,8,16,4]{3,2,1,0:T(8,128)S(1)} %get-tuple-element.68), channel_id=1, source_target_pairs={{0,4},{4,8},{8,12},{12,16},{16,20},{20,24},{24,28},{1,5},{5,9},{9,... | collective-permute-start | bytes 12296 | tf_op jit(solution)/shard_map/ppermute | solution.py:15
  145.6 1.9 %collective-permute-start.8 = (f32[2,8,16,4]{3,2,1,0:T(8,128)S(1)}, f32[2,8,16,4]{3,2,1,0:T(8,128)S(1)}, u32[]{:S(2)}, u32[]{:S(2)}) collective-permute-start(f32[2,8,16,4]{3,2,1,0:T(8,128)S(1)} %get-tuple-element.69), channel_id=1, source_target_pairs={{4,0},{8,4},{12,8},{16,12},{20,16},{24,20},{28,24},{5,1},{9,5},{13... | collective-permute-start | bytes 12296 | tf_op jit(solution)/shard_map/ppermute | solution.py:18
  147.7 5.8 %collective-permute-done.8 = f32[2,8,16,4]{3,2,1,0:T(8,128)S(1)} collective-permute-done((f32[2,8,16,4]{3,2,1,0:T(8,128)S(1)}, f32[2,8,16,4]{3,2,1,0:T(8,128)S(1)}, u32[]{:S(2)}, u32[]{:S(2)}) %collective-permute-start.8) | collective-permute-done | bytes 4128 | tf_op jit(solution)/shard_map/ppermute | solution.py:18
  153.5 0.2 pad_maximum_fusion.5
  153.7 3.6 %collective-permute-start.10 = (f32[2,4,16,136]{3,2,1,0:T(8,128)S(1)}, f32[2,4,16,136]{3,2,1,0:T(8,128)S(1)}, u32[]{:S(2)}, u32[]{:S(2)}) collective-permute-start(f32[2,4,16,136]{3,2,1,0:T(8,128)S(1)} %get-tuple-element.58), channel_id=1, source_target_pairs={{1,0},{2,1},{3,2},{5,4},{6,5},{7,6},{9,8},{10,9},{11,10},{13,12},{... | collective-permute-start | bytes 208904 | tf_op jit(solution)/shard_map/ppermute | solution.py:18
  157.4 1.9 %collective-permute-start.11 = (f32[2,4,16,136]{3,2,1,0:T(8,128)S(1)}, f32[2,4,16,136]{3,2,1,0:T(8,128)S(1)}, u32[]{:S(2)}, u32[]{:S(2)}) collective-permute-start(f32[2,4,16,136]{3,2,1,0:T(8,128)S(1)} %get-tuple-element.59), channel_id=1, source_target_pairs={{0,1},{1,2},{2,3},{4,5},{5,6},{6,7},{8,9},{9,10},{10,11},{12,13},{... | collective-permute-start | bytes 208904 | tf_op jit(solution)/shard_map/ppermute | solution.py:15
  159.3 0.2 pad_maximum_fusion.4
  159.5 3.6 %collective-permute-done.11 = f32[2,4,16,136]{3,2,1,0:T(8,128)S(1)} collective-permute-done((f32[2,4,16,136]{3,2,1,0:T(8,128)S(1)}, f32[2,4,16,136]{3,2,1,0:T(8,128)S(1)}, u32[]{:S(2)}, u32[]{:S(2)}) %collective-permute-start.11) | collective-permute-done | bytes 69664 | tf_op jit(solution)/shard_map/ppermute | solution.py:15
  163.1 0.2 pad_maximum_fusion.1
  163.3 0.3 fusion.18
  163.8 0.6 add_subtract_fusion
  164.6 0.6 copy-done.10
  (73 shorter events, 2.0 us)
Async XLA Ops:
  0.6 36.7 %copy-start = (f32[256,256]{1,0:T(8,128)S(1)}, f32[256,256]{1,0:T(8,128)}, u32[]{:S(2)}) copy-start(f32[256,256]{1,0:T(8,128)} %param.36) | copy-start | bytes 786436
  4.2 19.5 %copy-start.3 = (f32[8,8,128]{2,1,0:T(8,128)S(1)}, f32[8,8,128]{2,1,0:T(8,128)}, u32[]{:S(2)}) copy-start(f32[8,8,128]{2,1,0:T(8,128)} %param.25) | copy-start | bytes 98308
  4.2 19.5 %copy-start.4 = (f32[8,8,128]{2,1,0:T(8,128)S(1)}, f32[8,8,128]{2,1,0:T(8,128)}, u32[]{:S(2)}) copy-start(f32[8,8,128]{2,1,0:T(8,128)} %param.27) | copy-start | bytes 98308
  4.2 37.0 %all-to-all-start = ((s32[128,1,4]{2,1,0:T(1,128)}), s32[128,1,4]{2,1,0:T(1,128)S(1)}, u32[]{:S(2)}, u32[]{:S(2)}) async-start(s32[128,1,4]{2,1,0:T(1,128)} %bitcast.9), calls=%async_computation | async-start | bytes 131072 | tf_op jit(solution)/shard_map/all_to_all | solution.py:170
  23.7 13.4 %copy-start.12 = (f32[8,8,128]{2,1,0:T(8,128)S(1)}, f32[8,8,128]{2,1,0:T(8,128)}, u32[]{:S(2)}) copy-start(f32[8,8,128]{2,1,0:T(8,128)} %param.33) | copy-start | bytes 98308
  23.7 13.4 %copy-start.13 = (f32[8,8,128]{2,1,0:T(8,128)S(1)}, f32[8,8,128]{2,1,0:T(8,128)}, u32[]{:S(2)}) copy-start(f32[8,8,128]{2,1,0:T(8,128)} %param.32) | copy-start | bytes 98308
  23.7 13.2 %copy-start.17 = (s32[256]{0:T(256)S(1)}, s32[256]{0:T(256)}, u32[]{:S(2)}) copy-start(s32[256]{0:T(256)} %param.41) | copy-start | bytes 3076
  23.8 13.2 %copy-start.18 = (f32[64]{0:T(128)S(1)}, f32[64]{0:T(128)}, u32[]{:S(2)}) copy-start(f32[64]{0:T(128)} %param.38) | copy-start | bytes 772
  23.8 71.4 %collective-permute-start.1 = (f32[2,8,4,128]{3,2,1,0:T(4,128)S(1)}, f32[2,8,4,128]{3,2,1,0:T(4,128)S(1)}, u32[]{:S(2)}, u32[]{:S(2)}) collective-permute-start(f32[2,8,4,128]{3,2,1,0:T(4,128)S(1)} %get-tuple-element.85), channel_id=1, source_target_pairs={{0,32},{32,64},{64,96},{96,128},{128,160},{160,192},{192,224},{224... | collective-permute-start | bytes 98312 | tf_op jit(solution)/shard_map/ppermute | solution.py:15
  35.0 60.2 %collective-permute-start = (f32[2,8,4,128]{3,2,1,0:T(4,128)S(1)}, f32[2,8,4,128]{3,2,1,0:T(4,128)S(1)}, u32[]{:S(2)}, u32[]{:S(2)}) collective-permute-start(f32[2,8,4,128]{3,2,1,0:T(4,128)S(1)} %get-tuple-element.86), channel_id=1, source_target_pairs={{32,0},{64,32},{96,64},{128,96},{160,128},{192,160},{224,192},{256... | collective-permute-start | bytes 98312 | tf_op jit(solution)/shard_map/ppermute | solution.py:18
  37.3 0.7 copy-start.16
  41.2 32.8 %all-to-all-start.1 = ((f32[128,4,2]{1,2,0:T(2,128)}), f32[128,4,2]{1,2,0:T(2,128)S(1)}, u32[]{:S(2)}, u32[]{:S(2)}) async-start(f32[128,4,2]{1,2,0:T(2,128)} %copy.40), calls=%async_computation.1 | async-start | bytes 262144 | tf_op jit(solution)/shard_map/all_to_all | solution.py:169
  95.4 5.7 %collective-permute-start.3 = (f32[2,8,16,4]{3,2,1,0:T(8,128)S(1)}, f32[2,8,16,4]{3,2,1,0:T(8,128)S(1)}, u32[]{:S(2)}, u32[]{:S(2)}) collective-permute-start(f32[2,8,16,4]{3,2,1,0:T(8,128)S(1)} %get-tuple-element.72), channel_id=1, source_target_pairs={{0,4},{4,8},{8,12},{12,16},{16,20},{20,24},{24,28},{1,5},{5,9},{9,... | collective-permute-start | bytes 12296 | tf_op jit(solution)/shard_map/ppermute | solution.py:15
  98.8 6.0 %collective-permute-start.2 = (f32[2,8,16,4]{3,2,1,0:T(8,128)S(1)}, f32[2,8,16,4]{3,2,1,0:T(8,128)S(1)}, u32[]{:S(2)}, u32[]{:S(2)}) collective-permute-start(f32[2,8,16,4]{3,2,1,0:T(8,128)S(1)} %get-tuple-element.73), channel_id=1, source_target_pairs={{4,0},{8,4},{12,8},{16,12},{20,16},{24,20},{28,24},{5,1},{9,5},{13... | collective-permute-start | bytes 12296 | tf_op jit(solution)/shard_map/ppermute | solution.py:18
  105.0 5.7 %collective-permute-start.4 = (f32[2,4,16,136]{3,2,1,0:T(8,128)S(1)}, f32[2,4,16,136]{3,2,1,0:T(8,128)S(1)}, u32[]{:S(2)}, u32[]{:S(2)}) collective-permute-start(f32[2,4,16,136]{3,2,1,0:T(8,128)S(1)} %get-tuple-element.60), channel_id=1, source_target_pairs={{1,0},{2,1},{3,2},{5,4},{6,5},{7,6},{9,8},{10,9},{11,10},{13,12},{... | collective-permute-start | bytes 208904 | tf_op jit(solution)/shard_map/ppermute | solution.py:18
  107.0 6.3 %collective-permute-start.5 = (f32[2,4,16,136]{3,2,1,0:T(8,128)S(1)}, f32[2,4,16,136]{3,2,1,0:T(8,128)S(1)}, u32[]{:S(2)}, u32[]{:S(2)}) collective-permute-start(f32[2,4,16,136]{3,2,1,0:T(8,128)S(1)} %get-tuple-element.61), channel_id=1, source_target_pairs={{0,1},{1,2},{2,3},{4,5},{5,6},{6,7},{8,9},{9,10},{10,11},{12,13},{... | collective-permute-start | bytes 208904 | tf_op jit(solution)/shard_map/ppermute | solution.py:15
  114.1 0.8 copy-start.5
  114.1 0.8 copy-start.6
  114.1 0.8 copy-start.7
  114.1 0.8 copy-start.8
  114.1 0.8 copy-start.9
  114.1 0.8 copy-start.14
  114.1 0.8 copy-start.15
  115.0 49.5 %copy-start.1 = (f32[8,8,128]{2,1,0:T(8,128)}, f32[8,8,128]{2,1,0:T(8,128)S(1)}, u32[]{:S(2)}) copy-start(f32[8,8,128]{2,1,0:T(8,128)S(1)} %get-tuple-element.94) | copy-start | bytes 98308
  115.0 49.5 %copy-start.2 = (f32[8,8,128]{2,1,0:T(8,128)}, f32[8,8,128]{2,1,0:T(8,128)S(1)}, u32[]{:S(2)}) copy-start(f32[8,8,128]{2,1,0:T(8,128)S(1)} %get-tuple-element.95) | copy-start | bytes 98308
  115.0 12.5 %collective-permute-start.7 = (f32[2,8,4,128]{3,2,1,0:T(4,128)S(1)}, f32[2,8,4,128]{3,2,1,0:T(4,128)S(1)}, u32[]{:S(2)}, u32[]{:S(2)}) collective-permute-start(f32[2,8,4,128]{3,2,1,0:T(4,128)S(1)} %get-tuple-element.76), channel_id=1, source_target_pairs={{0,32},{32,64},{64,96},{96,128},{128,160},{160,192},{192,224},{224... | collective-permute-start | bytes 98312 | tf_op jit(solution)/shard_map/ppermute | solution.py:15
  125.6 16.1 %collective-permute-start.6 = (f32[2,8,4,128]{3,2,1,0:T(4,128)S(1)}, f32[2,8,4,128]{3,2,1,0:T(4,128)S(1)}, u32[]{:S(2)}, u32[]{:S(2)}) collective-permute-start(f32[2,8,4,128]{3,2,1,0:T(4,128)S(1)} %get-tuple-element.77), channel_id=1, source_target_pairs={{32,0},{64,32},{96,64},{128,96},{160,128},{192,160},{224,192},{256... | collective-permute-start | bytes 98312 | tf_op jit(solution)/shard_map/ppermute | solution.py:18
  141.8 5.9 %collective-permute-start.9 = (f32[2,8,16,4]{3,2,1,0:T(8,128)S(1)}, f32[2,8,16,4]{3,2,1,0:T(8,128)S(1)}, u32[]{:S(2)}, u32[]{:S(2)}) collective-permute-start(f32[2,8,16,4]{3,2,1,0:T(8,128)S(1)} %get-tuple-element.68), channel_id=1, source_target_pairs={{0,4},{4,8},{8,12},{12,16},{16,20},{20,24},{24,28},{1,5},{5,9},{9,... | collective-permute-start | bytes 12296 | tf_op jit(solution)/shard_map/ppermute | solution.py:15
  145.6 7.9 %collective-permute-start.8 = (f32[2,8,16,4]{3,2,1,0:T(8,128)S(1)}, f32[2,8,16,4]{3,2,1,0:T(8,128)S(1)}, u32[]{:S(2)}, u32[]{:S(2)}) collective-permute-start(f32[2,8,16,4]{3,2,1,0:T(8,128)S(1)} %get-tuple-element.69), channel_id=1, source_target_pairs={{4,0},{8,4},{12,8},{16,12},{20,16},{24,20},{28,24},{5,1},{9,5},{13... | collective-permute-start | bytes 12296 | tf_op jit(solution)/shard_map/ppermute | solution.py:18
  153.7 5.8 %collective-permute-start.10 = (f32[2,4,16,136]{3,2,1,0:T(8,128)S(1)}, f32[2,4,16,136]{3,2,1,0:T(8,128)S(1)}, u32[]{:S(2)}, u32[]{:S(2)}) collective-permute-start(f32[2,4,16,136]{3,2,1,0:T(8,128)S(1)} %get-tuple-element.58), channel_id=1, source_target_pairs={{1,0},{2,1},{3,2},{5,4},{6,5},{7,6},{9,8},{10,9},{11,10},{13,12},{... | collective-permute-start | bytes 208904 | tf_op jit(solution)/shard_map/ppermute | solution.py:18
  157.4 5.7 %collective-permute-start.11 = (f32[2,4,16,136]{3,2,1,0:T(8,128)S(1)}, f32[2,4,16,136]{3,2,1,0:T(8,128)S(1)}, u32[]{:S(2)}, u32[]{:S(2)}) collective-permute-start(f32[2,4,16,136]{3,2,1,0:T(8,128)S(1)} %get-tuple-element.59), channel_id=1, source_target_pairs={{0,1},{1,2},{2,3},{4,5},{5,6},{6,7},{8,9},{9,10},{10,11},{12,13},{... | collective-permute-start | bytes 208904 | tf_op jit(solution)/shard_map/ppermute | solution.py:15
  164.5 0.6 copy-start.10
  164.5 0.6 copy-start.11
where the time goes:
time: 166 us; the launch traced here: 165 us
  starting transfers between devices  84.1 us (51%)
  waiting for transfers between devices  44.7 us (27%)
  blocking collectives  17.4 us (10%)
  local copies, waits for them, and re-layouts  9.15 us (6%)
  other arithmetic  8.34 us (5%)
    ppermute x6, starting transfers between devices, with_halo(): lax.ppermute(lax.slice_in_dim(block, block.shape[dim] - width, None, axis...  34.4 us
    ppermute x6, waiting for transfers between devices, with_halo(): lax.ppermute(lax.slice_in_dim(block, 0, width, axis=dim), axis, backward)  23.6 us
    all_to_all x1, starting transfers between devices, local(): lax.all_to_all(label_buffer, ('inl', 'xl'), split_axis=0, concat_axis=0,...  19.5 us
    psum x1, blocking collectives, local(): planes = lax.psum(planes, 'gz')  17.4 us
    all_to_all x1, starting transfers between devices, local(): lax.all_to_all(float_buffer, ('inl', 'xl'), split_axis=0, concat_axis=0,...  16.9 us
    all_to_all x1, waiting for transfers between devices, local(): lax.all_to_all(float_buffer, ('inl', 'xl'), split_axis=0, concat_axis=0,...  14.5 us
    ppermute x6, starting transfers between devices, with_halo(): lax.ppermute(lax.slice_in_dim(block, 0, width, axis=dim), axis, backward)  13.2 us
    ppermute x6, waiting for transfers between devices, with_halo(): lax.ppermute(lax.slice_in_dim(block, block.shape[dim] - width, None, axis...  6.64 us
  transfers between devices with their start and end apart: 14, of which 8 were waited for; matrix products, arithmetic and copies ran while one was open for 6% of the time, Pallas kernels for 0%

commit v1 on v0

v1 whole, which is shorter than its diff:
```python
import functools

import jax
import jax.numpy as jnp
from jax import lax
from jax.experimental import pallas as pl
from jax.experimental.pallas import tpu as pltpu
from jax.sharding import PartitionSpec as P

MESH = pl.DeviceIdType.MESH
second_coef = (-205.0 / 72.0, 8.0 / 5.0, -1.0 / 5.0, 8.0 / 315.0, -1.0 / 560.0)
first_coef = (0.0, 4.0 / 5.0, -1.0 / 5.0, 4.0 / 105.0, -1.0 / 280.0)

OFFSETS = (
    [(d, 0, 0) for d in (1, -1)]
    + [(d, 0, e) for d in (1, -1) for e in (1, -1)]
    + [(d, e, 0) for d in (1, -1) for e in (1, -1)]
    + [(0, d, e) for d in (1, -1) for e in (1, -1)]
    + [(0, d, 0) for d in (1, -1)]
    + [(0, 0, d) for d in (1, -1)]
)
RING = 16
GROUP = 8
SLOTS = 4
WORDS = 16


def iota(shape, axis):
    return lax.broadcasted_iota(jnp.int32, shape, axis)


def shifted(body, halo, axis):
    size = body.shape[axis]
    place = iota(body.shape, axis)
    above = [pltpu.roll(jnp.where(place < k, halo, body), size - k, axis) for k in range(1, 5)]
    below = [pltpu.roll(jnp.where(place >= size - k, halo, body), k, axis) for k in range(1, 5)]
    return above, below


def slope(above, below):
    total = first_coef[1] * (above[0] - below[0])
    for k in range(2, 5):
        total = total + first_coef[k] * (above[k - 1] - below[k - 1])
    return total


def bend(center, above, below):
    total = second_coef[0] * center
    for k in range(1, 5):
        total = total + second_coef[k] * (above[k - 1] + below[k - 1])
    return total


def kernel(sizes, *refs):
    n_inl, n_xl, n_gz = sizes
    (
        wave_p,
        wave_p_old,
        wave_q,
        wave_q_old,
        courant,
        epsilon,
        delta,
        tilt,
        azimuth,
        shear,
        damping,
        samples,
        weights,
        gain,
        inline,
        crossline,
        shot,
        next_p,
        next_q,
        prior_p,
        prior_q,
        body,
        side,
        packed,
        parcel,
        edge_y,
        edge_xy,
        old,
        field,
        coef,
        trace,
        small_w,
        small_g,
        small_r,
        letters,
        mail,
        bundle,
        heap,
        plane,
        result,
        load_sem,
        store_sem,
        send_sem,
        recv_sem,
        letter_send,
        letter_recv,
        bundle_send,
        bundle_recv,
    ) = refs
    i = lax.axis_index("inl")
    j = lax.axis_index("xl")
    g = lax.axis_index("gz")
    depth, across, along = 8, 8, 128
    half = n_inl // 2
    ring = 2 * n_xl
    high, low = i // half, i % half
    level = high * n_xl + j

    loads = [
        (wave_p, body.at[0, 0, pl.ds(4, depth)]),
        (wave_q, body.at[0, 1, pl.ds(4, depth)]),
        (wave_p_old, old.at[0]),
        (wave_q_old, old.at[1]),
        (courant, field.at[0]),
        (epsilon, field.at[1]),
        (delta, field.at[2]),
        (tilt, field.at[3]),
        (azimuth, field.at[4]),
        (shear, field.at[5]),
        (damping, field.at[6]),
        (samples, trace),
        (weights, small_w),
        (gain, small_g),
        (inline, small_r.at[0]),
        (crossline, small_r.at[1]),
        (shot, small_r.at[2]),
    ]
    loads = [pltpu.make_async_copy(a, b, load_sem.at[k]) for k, (a, b) in enumerate(loads)]
    for copy in loads:
        copy.start()

    nothing = jnp.zeros((2, 4, across, along), jnp.float32)
    for turn in range(2):
        body[turn, :, 0:4] = nothing
        body[turn, :, 12:16] = nothing
        for k in range(4):
            side[turn, :, 4 * k : 4 * k + 4] = nothing
        packed[turn] = jnp.zeros((5, 2, across, along), jnp.float32)
    mail[...] = jnp.zeros((RING, along), jnp.float32)
    heap[...] = jnp.zeros((4, 2, GROUP, along), jnp.float32)

    def there(offset):
        d, e, f = offset
        ok = []
        for step, place, count in ((d, i, n_inl), (e, j, n_xl), (f, g, n_gz)):
            if step == 1:
                ok.append(place < count - 1)
            if step == -1:
                ok.append(place > 0)
        return functools.reduce(jnp.logical_and, ok)

    def device(offset):
        d, e, f = offset
        return (
            jnp.clip(i + d, 0, n_inl - 1),
            jnp.clip(j + e, 0, n_xl - 1),
            jnp.clip(g + f, 0, n_gz - 1),
        )

    def on_ring(k):
        place = lax.rem(level + k, ring)
        return (place // n_xl * half + low, lax.rem(place, n_xl), g)

    def in_group(k, layer):
        return (high * half + lax.rem(low + k, half), j, layer)

    barrier = pltpu.get_barrier_semaphore()
    count = jnp.int32(ring - 1) + jnp.where(g == 0, half - 1, half)
    for offset in OFFSETS:

        @pl.when(there(offset))
        def _(offset=offset):
            pl.semaphore_signal(barrier, inc=1, device_id=device(offset), device_id_type=MESH)

        count = count + there(offset).astype(jnp.int32)
    for k in range(1, ring):
        pl.semaphore_signal(barrier, inc=1, device_id=on_ring(k), device_id_type=MESH)

    @pl.when(g == 0)
    def _():
        for layer in range(n_gz):
            for k in range(half):
                if layer > 0 or k > 0:
                    pl.semaphore_signal(
                        barrier, inc=1, device_id=in_group(k, layer), device_id_type=MESH
                    )

    for copy in loads:
        copy.wait()

    def prepare(z, _):
        sin_t, cos_t = jnp.sin(field[3, z]), jnp.cos(field[3, z])
        sin_f, cos_f = jnp.sin(field[4, z]), jnp.cos(field[4, z])
        coef[0, z] = sin_t * sin_t * cos_f * cos_f
        coef[1, z] = sin_t * sin_t * sin_f * sin_f
        coef[2, z] = cos_t * cos_t
        coef[3, z] = 2.0 * sin_t * sin_t * sin_f * cos_f
        coef[4, z] = 2.0 * sin_t * cos_t * cos_f
        coef[5, z] = 2.0 * sin_t * cos_t * sin_f
        c, s = field[0, z], field[5, z]
        grow, lean = 1.0 + 2.0 * field[1, z], 1.0 + 2.0 * field[2, z]
        coef[6, z] = c * grow
        coef[7, z] = c * (s - grow)
        coef[8, z] = c * (1.0 - s)
        coef[9, z] = c * (lean - s)
        coef[10, z] = c * s
        coef[11, z] = 1.0 - field[6, z]
        return 0

    lax.fori_loop(0, depth, prepare, 0)

    n_traces = trace.shape[0]
    row, column, line = small_r[0], small_r[1], small_r[2]
    lines = small_g.shape[1]
    picked = jnp.where(iota((lines, n_traces), 0) == line, 1.0, 0.0).astype(jnp.float32)
    gains = jnp.dot(
        small_g[...],
        picked,
        precision=lax.Precision.HIGHEST,
        preferred_element_type=jnp.float32,
    )
    amplitude = (
        lax.dot_general(
            small_w[...],
            trace[...],
            (((1,), (1,)), ((), ())),
            precision=lax.Precision.HIGHEST,
            preferred_element_type=jnp.float32,
        )
        * gains
    )
    to_inl, to_xl = row >> 3, column >> 7
    cell = ((row & 7) << 7) + (column & 127) + 1
    to_high = jnp.where(to_inl >= half, 1, 0)
    to_low = to_inl - to_high * half
    owner = to_inl * n_xl + to_xl
    columns = n_inl * n_xl
    member = jnp.where(iota((columns, n_traces), 0) == owner, 1.0, 0.0).astype(jnp.float32)
    earlier = jnp.where(
        iota((n_traces, n_traces), 0) < iota((n_traces, n_traces), 1), 1.0, 0.0
    ).astype(jnp.float32)
    before = jnp.dot(
        member.astype(jnp.bfloat16),
        earlier.astype(jnp.bfloat16),
        preferred_element_type=jnp.float32,
    )
    rank = jnp.sum(member * before, axis=0, keepdims=True).astype(jnp.int32)
    hop = to_high * n_xl + to_xl - level
    hop = jnp.where(hop < 0, hop + ring, hop)
    block = to_low - low
    block = jnp.where(block < 0, block + half, block)
    word = block * WORDS + rank
    spot = iota((along, n_traces), 0)
    content = (
        jnp.where(spot == word, amplitude[0:1, :], 0.0)
        + jnp.where(spot == word + SLOTS, amplitude[1:2, :], 0.0)
        + jnp.where(spot == word + 2 * SLOTS, cell.astype(jnp.float32), 0.0)
    )
    address = jnp.where(iota((RING, n_traces), 0) == hop, 1.0, 0.0).astype(jnp.float32)
    written = lax.dot_general(
        address,
        content,
        (((1,), (1,)), ((), ())),
        precision=lax.Precision.HIGHEST,
        preferred_element_type=jnp.float32,
    )
    letters[...] = written
    mail[0:1, :] = written[0:1, :]

    lane = iota((across, along), 1)
    sub = iota((across, along), 0)

    def pack(turn):
        total = jnp.zeros((across, along), jnp.float32)
        for f in range(2):
            for z in range(depth):
                tile = f * depth + z
                moved = pltpu.roll(body[turn, f, 4 + z], (8 * tile + 4) % along, 1)
                total = jnp.where(lane // 8 == tile, moved, total)
        parcel[turn] = total

    pack(0)

    def copies(turn):
        out = []
        mine = body.at[turn]
        beside = side.at[turn]
        for number, offset in enumerate(OFFSETS):
            d, e, f = offset
            if e != 0:
                kind = 0
                if f != 0:
                    kind = 1 if f == 1 else 2
                if d != 0:
                    kind = 3 if d == 1 else 4
                source = parcel.at[turn]
                target = packed.at[turn, kind, 0 if e == 1 else 1]
            else:
                deep = {0: (4, 8, 4), 1: (8, 4, 0), -1: (4, 4, 12)}[f]
                if d == 0:
                    source = mine.at[:, pl.ds(deep[0], deep[1])]
                    target = mine.at[:, pl.ds(deep[2], deep[1])]
                else:
                    wide = pl.ds(4 if d == 1 else 0, 4)
                    source = mine.at[:, pl.ds(deep[0], deep[1]), wide]
                    target = beside.at[:, pl.ds(deep[2], deep[1]), wide]
            out.append(
                pltpu.make_async_remote_copy(
                    src_ref=source,
                    dst_ref=target,
                    send_sem=send_sem.at[turn, number],
                    recv_sem=recv_sem.at[turn, number],
                    device_id=device(offset),
                    device_id_type=MESH,
                )
            )
        return out

    def begin(turn):
        for offset, copy in zip(OFFSETS, copies(turn)):

            @pl.when(there(offset))
            def _(copy=copy):
                copy.start()

    def arrive(turn):
        for offset, copy in zip(OFFSETS, copies(turn)):

            @pl.when(there(tuple(-d for d in offset)))
            def _(copy=copy):
                copy.wait_recv()

    def depart(turn):
        for offset, copy in zip(OFFSETS, copies(turn)):

            @pl.when(there(offset))
            def _(copy=copy):
                copy.wait_send()

    def letter(k):
        return pltpu.make_async_remote_copy(
            src_ref=letters.at[pl.ds(k, 1)],
            dst_ref=mail.at[pl.ds(k, 1)],
            send_sem=letter_send.at[k],
            recv_sem=letter_recv.at[k],
            device_id=on_ring(k),
            device_id_type=MESH,
        )

    def parcel_of(k, layer):
        return pltpu.make_async_remote_copy(
            src_ref=bundle.at[:, pl.ds(k, 1)],
            dst_ref=heap.at[layer, :, pl.ds(k, 1)],
            send_sem=bundle_send.at[k],
            recv_sem=bundle_recv.at[layer, k],
            device_id=in_group(k, 0),
            device_id_type=MESH,
        )

    pl.semaphore_wait(barrier, count)
    begin(0)
    for k in range(1, ring):
        letter(k).start()

    for k in range(1, ring):
        letter(k).wait_recv()
    for t in range(2):
        got = mail[8 * t : 8 * t + 8, :]
        turned = jnp.zeros((GROUP, along), jnp.float32)
        for d in range(GROUP):
            moved = got if d == 0 else pltpu.roll(pltpu.roll(got, d, 0), along - WORDS * d, 1)
            turned = jnp.where(((sub - lane // WORDS) & 7) == d, moved, turned)
        bundle[t] = turned

    for k in range(half):
        if k > 0:
            parcel_of(k, g).start()
        else:

            @pl.when(g > 0)
            def _():
                parcel_of(0, g).start()

            @pl.when(g == 0)
            def _():
                heap[0, :, 0:1] = bundle[:, 0:1]

    def unpack(turn):
        def pair(kind):
            return jnp.where(lane % 8 < 4, packed[turn, kind, 0], packed[turn, kind, 1])

        plain = pair(0)
        deep = jnp.where((lane // 8) % 8 >= 4, pair(1), pair(2))
        wide = jnp.where(sub < 4, pair(4), pair(3))
        for f in range(2):
            for z in range(depth):
                turnback = (along - 4 - 8 * (f * depth + z)) % along
                edge_y[f, 4 + z] = pltpu.roll(plain, turnback, 1)
                edge_y[f, z - 4 if z >= 4 else 12 + z] = pltpu.roll(deep, turnback, 1)
                edge_xy[f, z] = pltpu.roll(wide, turnback, 1)

    def advance(turn, store):
        def layer(z, _):
            first, whole = [], []
            for f in range(2):
                center = body[turn, f, z + 4]
                beside = side[turn, f, z + 4]
                edge = edge_y[f, z + 4]
                above = [body[turn, f, z + 4 + k] for k in range(1, 5)]
                below = [body[turn, f, z + 4 - k] for k in range(1, 5)]
                u_zz = bend(center, above, below)
                grad_z = slope(above, below)
                grad_z_side = slope(
                    [side[turn, f, z + 4 + k] for k in range(1, 5)],
                    [side[turn, f, z + 4 - k] for k in range(1, 5)],
                )
                grad_z_edge = slope(
                    [edge_y[f, z + 4 + k] for k in range(1, 5)],
                    [edge_y[f, z + 4 - k] for k in range(1, 5)],
                )
                x_moves = shifted(center, beside, 0)
                u_xx = bend(center, *x_moves)
                grad_x = slope(*x_moves)
                grad_x_edge = slope(*shifted(edge, edge_xy[f, z], 0))
                u_yy = bend(center, *shifted(center, edge, 1))
                u_xy = slope(*shifted(grad_x, grad_x_edge, 1))
                u_xz = slope(*shifted(grad_z, grad_z_side, 0))
                u_yz = slope(*shifted(grad_z, grad_z_edge, 1))
                first.append(
                    coef[0, z] * u_xx
                    + coef[1, z] * u_yy
                    + coef[2, z] * u_zz
                    + coef[3, z] * u_xy
                    + coef[4, z] * u_xz
                    + coef[5, z] * u_yz
                )
                whole.append(u_xx + u_yy + u_zz)
            stay = coef[11, z]
            now_p, now_q = body[turn, 0, z + 4], body[turn, 1, z + 4]
            if turn == 0:
                was_p, was_q = old[0, z], old[1, z]
            else:
                was_p, was_q = body[0, 0, z + 4], body[0, 1, z + 4]
            mixed = coef[8, z] * first[1]
            new_p = (
                now_p
                + stay * (now_p - was_p)
                + (coef[6, z] * whole[0] + coef[7, z] * first[0] + mixed)
            )
            new_q = (
                now_q
                + stay * (now_q - was_q)
                + (coef[9, z] * (whole[0] - first[0]) + coef[10, z] * whole[1] + mixed)
            )
            store(z, new_p, new_q)
            return 0

        lax.fori_loop(0, depth, layer, 0)

    def keep(z, new_p, new_q):
        body[1, 0, z + 4] = new_p
        body[1, 1, z + 4] = new_q

    def finish(z, new_p, new_q):
        result[0, z] = new_p
        result[1, z] = new_q

    arrive(0)
    unpack(0)
    advance(0, keep)

    @pl.when(g == 0)
    def _():
        for layer in range(n_gz):
            for k in range(half):
                if layer > 0 or k > 0:
                    parcel_of(k, layer).wait_recv()
        place = iota((2 * GROUP, along), 1) % WORDS // SLOTS
        parts = [heap[layer].reshape(2 * GROUP, along) for layer in range(4)]

        def gather(kind):
            total = jnp.zeros((2 * GROUP, along), jnp.float32)
            for layer in range(4):
                shift = SLOTS * (layer - kind) % along
                moved = parts[layer] if shift == 0 else pltpu.roll(parts[layer], shift, 1)
                total = jnp.where(place == layer, moved, total)
            return total

        label = gather(2).astype(jnp.int32) - 1
        label_x, label_y = label >> 7, label & 127
        pieces = []
        for kind in range(2):
            rest = gather(kind)
            for _ in range(3):
                rounded = rest.astype(jnp.bfloat16).astype(jnp.float32)
                pieces.append(rounded)
                rest = rest - rounded
        total = jnp.zeros((6 * across, along), jnp.float32)
        for r in range(0, 2 * GROUP, 2):

            def flat(array):
                return jnp.concatenate([array[r : r + 1], array[r + 1 : r + 2]], axis=1)

            at_x = iota((across, 2 * along), 0) == flat(label_x)
            left = jnp.concatenate(
                [jnp.where(at_x, flat(piece), 0.0) for piece in pieces], axis=0
            )
            right = jnp.where(iota((along, 2 * along), 0) == flat(label_y), 1.0, 0.0)
            total = total + lax.dot_general(
                left.astype(jnp.bfloat16),
                right.astype(jnp.bfloat16),
                (((1,), (1,)), ((), ())),
                preferred_element_type=jnp.float32,
            )
        for k in range(2):
            part = total[24 * k : 24 * k + 24]
            plane[k] = part[0:8] + part[8:16] + part[16:24]
        for f in range(2):
            body[1, f, 4] = body[1, f, 4] + plane[0]

    pack(1)
    begin(1)
    stores = [
        pltpu.make_async_copy(body.at[1, 0, pl.ds(4, depth)], prior_p, store_sem.at[0]),
        pltpu.make_async_copy(body.at[1, 1, pl.ds(4, depth)], prior_q, store_sem.at[1]),
        pltpu.make_async_copy(result.at[0], next_p, store_sem.at[2]),
        pltpu.make_async_copy(result.at[1], next_q, store_sem.at[3]),
    ]
    stores[0].start()
    stores[1].start()
    arrive(1)
    unpack(1)
    advance(1, finish)

    @pl.when(g == 0)
    def _():
        for f in range(2):
            result[f, 0] = result[f, 0] + plane[1]

    stores[2].start()
    stores[3].start()
    depart(0)
    depart(1)
    for k in range(1, ring):
        letter(k).wait_send()
    for k in range(half):
        if k > 0:
            parcel_of(k, g).wait_send()
        else:

            @pl.when(g > 0)
            def _():
                parcel_of(0, g).wait_send()

    for copy in stores:
        copy.wait()


def local(sizes, *args):
    fields = args[:11]
    samples, weights, gain, row, column, line = args[11:]
    block = fields[0].shape
    n_traces = samples.shape[0]
    receivers = [ids.reshape(1, -1) for ids in (row, column, line)]
    f32 = jnp.float32
    return pl.pallas_call(
        functools.partial(kernel, sizes),
        out_shape=[jax.ShapeDtypeStruct(block, f32)] * 4,
        in_specs=[pl.BlockSpec(memory_space=pltpu.HBM)] * 17,
        out_specs=[pl.BlockSpec(memory_space=pltpu.HBM)] * 4,
        scratch_shapes=[
            pltpu.VMEM((2, 2, 16, 8, 128), f32),
            pltpu.VMEM((2, 2, 16, 8, 128), f32),
            pltpu.VMEM((2, 5, 2, 8, 128), f32),
            pltpu.VMEM((2, 8, 128), f32),
            pltpu.VMEM((2, 16, 8, 128), f32),
            pltpu.VMEM((2, 8, 8, 128), f32),
            pltpu.VMEM((2, 8, 8, 128), f32),
            pltpu.VMEM((7, 8, 8, 128), f32),
            pltpu.VMEM((12, 8, 8, 128), f32),
            pltpu.VMEM(samples.shape, f32),
            pltpu.VMEM(weights.shape, f32),
            pltpu.VMEM((1, gain.shape[0]), f32),
            pltpu.VMEM((3, 1, n_traces), jnp.int32),
            pltpu.VMEM((RING, 128), f32),
            pltpu.VMEM((RING, 128), f32),
            pltpu.VMEM((2, GROUP, 128), f32),
            pltpu.VMEM((4, 2, GROUP, 128), f32),
            pltpu.VMEM((2, 8, 128), f32),
            pltpu.VMEM((2, 8, 8, 128), f32),
            pltpu.SemaphoreType.DMA((17,)),
            pltpu.SemaphoreType.DMA((4,)),
            pltpu.SemaphoreType.DMA((2, len(OFFSETS))),
            pltpu.SemaphoreType.DMA((2, len(OFFSETS))),
            pltpu.SemaphoreType.DMA((RING,)),
            pltpu.SemaphoreType.DMA((RING,)),
            pltpu.SemaphoreType.DMA((GROUP,)),
            pltpu.SemaphoreType.DMA((4, GROUP)),
        ],
        compiler_params=pltpu.CompilerParams(
            collective_id=0, has_side_effects=True, vmem_limit_bytes=60 * 2**20
        ),
        name="wave_steps",
    )(*fields, samples, weights, gain.reshape(1, -1), *receivers)


def solution(mesh):
    sizes = tuple(mesh.shape[axis] for axis in ("inl", "xl", "gz"))
    cells = P("gz", "inl", "xl")
    traces = P(("inl", "xl", "gz"))
    return jax.shard_map(
        functools.partial(local, sizes),
        mesh=mesh,
        in_specs=(cells,) * 11 + (P(("inl", "xl", "gz"), None), P(), P(), traces, traces, traces),
        out_specs=(cells,) * 4,
        check_vma=False,
    )
```

time: 166 us -> 47.3 us (0.28)
  the two profiles are of different devices: /device:TPU:61 before, /device:TPU:59 now
where the time goes in v1:
time: 47.3 us; the launch traced here: 47 us
  Pallas kernels  42.8 us (90%)
  local copies, waits for them, and re-layouts  3.54 us (7%)
  between operations  0.66 us (1%)
    pallas_call x1, Pallas kernels, local(): pl.pallas_call(functools.partial(kernel, sizes), out_shape=[jax.ShapeDtyp...  42.8 us
    unnamed x10, local copies, waits for them, and re-layouts  3.54 us

profile of v1, /device:TPU:59, one launch (start us, length us, event | category | flops | bytes accessed | tf_op | source)
XLA Modules:
  0.0 47.0 jit_solution(16755013539597353405)
XLA Ops:
  0.6 42.8 %wave_steps.1 = (f32[8,8,128]{2,1,0:T(8,128)}, f32[8,8,128]{2,1,0:T(8,128)}, f32[8,8,128]{2,1,0:T(8,128)}, f32[8,8,128]{2,1,0:T(8,128)}) custom-call(f32[8,8,128]{2,1,0:T(8,128)} %refs_0_.1, f32[8,8,128]{2,1,0:T(8,128)} %refs_1_.1, f32[8,8,128]{2,1,0:T(8,128)} %refs_2_.1, f32[8,8,128]{2,1,0:T(8,128)} %refs_3_.1, f32[8,8,128]{2,1,0:T(8,128)} %refs_4_.1, ...), custom_call_target="tpu_custom_call" | custom-call | tf_op jit(solution)/shard_map/wave_steps/pallas_call | solution.py:572
  43.4 0.0 copy-start.2
  43.5 1.4 %copy.25 = f32[8,8,128]{2,1,0:T(8,128)} copy(f32[8,8,128]{2,1,0:T(8,128)} %get-tuple-element.8) | data formatting | bytes 65536
  44.8 0.0 copy-done.2
  44.8 0.0 copy-start.1
  44.8 0.6 %copy.26 = f32[8,8,128]{2,1,0:T(8,128)} copy(f32[8,8,128]{2,1,0:T(8,128)S(1)} %copy-done.2) | data formatting | bytes 65536
  45.5 0.2 copy-done.1
  45.6 0.0 copy-start
  45.6 0.6 %copy.27 = f32[8,8,128]{2,1,0:T(8,128)} copy(f32[8,8,128]{2,1,0:T(8,128)S(1)} %copy-done.1) | data formatting | bytes 65536
  46.2 0.2 copy-done
  46.4 0.6 %copy.28 = f32[8,8,128]{2,1,0:T(8,128)} copy(f32[8,8,128]{2,1,0:T(8,128)S(1)} %copy-done) | data formatting | bytes 65536
Async XLA Ops:
  43.4 1.4 %copy-start.2 = (f32[8,8,128]{2,1,0:T(8,128)S(1)}, f32[8,8,128]{2,1,0:T(8,128)}, u32[]{:S(2)}) copy-start(f32[8,8,128]{2,1,0:T(8,128)} %get-tuple-element.9) | copy-start | bytes 98308
  44.8 0.8 %copy-start.1 = (f32[8,8,128]{2,1,0:T(8,128)S(1)}, f32[8,8,128]{2,1,0:T(8,128)}, u32[]{:S(2)}) copy-start(f32[8,8,128]{2,1,0:T(8,128)} %get-tuple-element.10) | copy-start | bytes 98308
  45.6 0.8 %copy-start = (f32[8,8,128]{2,1,0:T(8,128)S(1)}, f32[8,8,128]{2,1,0:T(8,128)}, u32[]{:S(2)}) copy-start(f32[8,8,128]{2,1,0:T(8,128)} %get-tuple-element.11) | copy-start | bytes 98308

commit v2 on v1

--- a/solution.py
+++ b/solution.py
@@ -23,6 +23,7 @@
 GROUP = 8
 SLOTS = 4
 WORDS = 16
+BESIDE = [(d, e) for d in (1, -1, 0) for e in (1, -1, 0) if d != 0 or e != 0]
 
 
 def iota(shape, axis):
@@ -89,10 +90,17 @@
         small_g,
         small_r,
         letters,
+        transit,
         mail,
         bundle,
+        bundle_far,
         heap,
+        heap_far,
         plane,
+        plane_far,
+        plane_side,
+        plane_parcel,
+        plane_packed,
         result,
         load_sem,
         store_sem,
@@ -100,8 +108,14 @@
         recv_sem,
         letter_send,
         letter_recv,
+        relay_send,
+        relay_recv,
         bundle_send,
         bundle_recv,
+        far_send,
+        far_recv,
+        plane_send,
+        plane_recv,
     ) = refs
     i = lax.axis_index("inl")
     j = lax.axis_index("xl")
@@ -111,6 +125,10 @@
     ring = 2 * n_xl
     high, low = i // half, i % half
     level = high * n_xl + j
+    quarter = ring // 4
+    border = jnp.where(high == 0, half - 1, 0)
+    on_border = low == border
+    surface = g == 0
 
     loads = [
         (wave_p, body.at[0, 0, pl.ds(4, depth)]),
@@ -142,8 +160,13 @@
         for k in range(4):
             side[turn, :, 4 * k : 4 * k + 4] = nothing
         packed[turn] = jnp.zeros((5, 2, across, along), jnp.float32)
-    mail[...] = jnp.zeros((RING, along), jnp.float32)
+    mail[...] = jnp.zeros((2, RING, along), jnp.float32)
     heap[...] = jnp.zeros((4, 2, GROUP, along), jnp.float32)
+    for layer in range(4):
+        heap_far[layer] = jnp.zeros((GROUP, across, along), jnp.float32)
+    plane_far[...] = jnp.zeros((across, along), jnp.float32)
+    plane_side[...] = jnp.zeros((across, along), jnp.float32)
+    plane_packed[...] = jnp.zeros((3, 2, across, along), jnp.float32)
 
     def there(offset):
         d, e, f = offset
@@ -164,14 +187,14 @@
         )
 
     def on_ring(k):
-        place = lax.rem(level + k, ring)
+        place = lax.rem(level + k + ring, ring)
         return (place // n_xl * half + low, lax.rem(place, n_xl), g)
 
     def in_group(k, layer):
         return (high * half + lax.rem(low + k, half), j, layer)
 
     barrier = pltpu.get_barrier_semaphore()
-    count = jnp.int32(ring - 1) + jnp.where(g == 0, half - 1, half)
+    count = jnp.int32(2 * quarter) + jnp.where(surface, half - 1, half)
     for offset in OFFSETS:
 
         @pl.when(there(offset))
@@ -179,10 +202,11 @@
             pl.semaphore_signal(barrier, inc=1, device_id=device(offset), device_id_type=MESH)
 
         count = count + there(offset).astype(jnp.int32)
-    for k in range(1, ring):
+    near_ring = [k for k in range(-quarter, quarter + 1) if k != 0]
+    for k in near_ring:
         pl.semaphore_signal(barrier, inc=1, device_id=on_ring(k), device_id_type=MESH)
 
-    @pl.when(g == 0)
+    @pl.when(surface)
     def _():
         for layer in range(n_gz):
             for k in range(half):
@@ -251,8 +275,7 @@
         preferred_element_type=jnp.float32,
     )
     rank = jnp.sum(member * before, axis=0, keepdims=True).astype(jnp.int32)
-    hop = to_high * n_xl + to_xl - level
-    hop = jnp.where(hop < 0, hop + ring, hop)
+    to_level = to_high * n_xl + to_xl
     block = to_low - low
     block = jnp.where(block < 0, block + half, block)
     word = block * WORDS + rank
@@ -262,16 +285,28 @@
         + jnp.where(spot == word + SLOTS, amplitude[1:2, :], 0.0)
         + jnp.where(spot == word + 2 * SLOTS, cell.astype(jnp.float32), 0.0)
     )
-    address = jnp.where(iota((RING, n_traces), 0) == hop, 1.0, 0.0).astype(jnp.float32)
-    written = lax.dot_general(
-        address,
-        content,
-        (((1,), (1,)), ((), ())),
-        precision=lax.Precision.HIGHEST,
-        preferred_element_type=jnp.float32,
+    leaves = (to_inl == half - 1) & ((row & 7) >= 4)
+    enters = (to_inl == half) & ((row & 7) < 4)
+    far_level = jnp.where(leaves, n_xl + to_xl, to_xl)
+    far_word = 2 * SLOTS * level + rank
+    far_content = jnp.where(spot == far_word, amplitude[0:1, :], 0.0) + jnp.where(
+        spot == far_word + SLOTS, cell.astype(jnp.float32), 0.0
     )
-    letters[...] = written
-    mail[0:1, :] = written[0:1, :]
+
+    def write(target, wanted, words):
+        hop = target - level + ring // 2
+        hop = jnp.where(hop < 0, hop + ring, jnp.where(hop >= ring, hop - ring, hop))
+        address = (iota((RING, n_traces), 0) == hop) & wanted
+        return lax.dot_general(
+            jnp.where(address, 1.0, 0.0).astype(jnp.float32),
+            words,
+            (((1,), (1,)), ((), ())),
+            precision=lax.Precision.HIGHEST,
+            preferred_element_type=jnp.float32,
+        )
+
+    letters[0] = write(to_level, to_level >= 0, content)
+    letters[1] = write(far_level, leaves | enters, far_content)
 
     lane = iota((across, along), 1)
     sub = iota((across, along), 0)
@@ -344,11 +379,27 @@
                 copy.wait_send()
 
     def letter(k):
+        rows = pl.ds(2 * (k + quarter), 2)
         return pltpu.make_async_remote_copy(
-            src_ref=letters.at[pl.ds(k, 1)],
-            dst_ref=mail.at[pl.ds(k, 1)],
-            send_sem=letter_send.at[k],
-            recv_sem=letter_recv.at[k],
+            src_ref=letters.at[:, rows],
+            dst_ref=transit.at[:, rows],
+            send_sem=letter_send.at[k + quarter],
+            recv_sem=letter_recv.at[k + quarter],
+            device_id=on_ring(k),
+            device_id_type=MESH,
+        )
+
+    def relay_rows(k):
+        first = max(2 * (k + quarter) - 1, 0)
+        return first, min(2 * (k + quarter) + 1, ring) - first
+
+    def relay(k):
+        rows = pl.ds(*relay_rows(k))
+        return pltpu.make_async_remote_copy(
+            src_ref=transit.at[:, rows],
+            dst_ref=mail.at[:, rows],
+            send_sem=relay_send.at[k + quarter],
+            recv_sem=relay_recv.at[k + quarter],
             device_id=on_ring(k),
             device_id_type=MESH,
         )
@@ -363,33 +414,61 @@
             device_id_type=MESH,
         )
 
+    def far_parcel(layer, place):
+        return pltpu.make_async_remote_copy(
+            src_ref=bundle_far,
+            dst_ref=heap_far.at[layer, place],
+            send_sem=far_send,
+            recv_sem=far_recv.at[layer, place],
+            device_id=(high * half + border, j, 0),
+            device_id_type=MESH,
+        )
+
+    def post():
+        for k in near_ring:
+            relay(k).wait_recv()
+        for t in range(2):
+            got = mail[0, 8 * t : 8 * t + 8, :]
+            turned = jnp.zeros((GROUP, along), jnp.float32)
+            for d in range(GROUP):
+                moved = got if d == 0 else pltpu.roll(pltpu.roll(got, d, 0), along - WORDS * d, 1)
+                turned = jnp.where(((sub - lane // WORDS) & 7) == d, moved, turned)
+            bundle[t] = turned
+        far = jnp.sum(mail[1], axis=0, keepdims=True)
+        bundle_far[...] = jnp.where(sub == low, far, 0.0)
+        for k in range(1, half):
+            parcel_of(k, g).start()
+
+        @pl.when(jnp.logical_not(surface))
+        def _():
+            parcel_of(0, g).start()
+
+        @pl.when(surface)
+        def _():
+            heap[0, :, 0:1] = bundle[:, 0:1]
+
+        @pl.when(jnp.logical_not(surface & on_border))
+        def _():
+            far_parcel(g, low).start()
+
+        @pl.when(surface & on_border)
+        def _():
+            heap_far[0, border] = bundle_far[...]
+
     pl.semaphore_wait(barrier, count)
     begin(0)
-    for k in range(1, ring):
-        letter(k).start()
-
-    for k in range(1, ring):
-        letter(k).wait_recv()
-    for t in range(2):
-        got = mail[8 * t : 8 * t + 8, :]
-        turned = jnp.zeros((GROUP, along), jnp.float32)
-        for d in range(GROUP):
-            moved = got if d == 0 else pltpu.roll(pltpu.roll(got, d, 0), along - WORDS * d, 1)
-            turned = jnp.where(((sub - lane // WORDS) & 7) == d, moved, turned)
-        bundle[t] = turned
-
-    for k in range(half):
-        if k > 0:
-            parcel_of(k, g).start()
-        else:
-
-            @pl.when(g > 0)
-            def _():
-                parcel_of(0, g).start()
-
-            @pl.when(g == 0)
-            def _():
-                heap[0, :, 0:1] = bundle[:, 0:1]
+    for k in range(-quarter, quarter):
+        if k != 0:
+            letter(k).start()
+    own = pl.ds(2 * quarter, 2)
+    transit[:, own] = letters[:, own]
+    for k in range(-quarter, quarter):
+        if k != 0:
+            letter(k).wait_recv()
+    for k in near_ring:
+        relay(k).start()
+    kept = pl.ds(*relay_rows(0))
+    mail[:, kept] = transit[:, kept]
 
     def unpack(turn):
         def pair(kind):
@@ -471,11 +550,75 @@
         result[0, z] = new_p
         result[1, z] = new_q
 
+    late = (high == 0) & on_border
+
+    @pl.when(late)
+    def _():
+        post()
+
     arrive(0)
     unpack(0)
     advance(0, keep)
-
-    @pl.when(g == 0)
+    pack(1)
+    begin(1)
+
+    @pl.when(jnp.logical_not(late))
+    def _():
+        post()
+
+    def add_up(label, values):
+        label_x, label_y = label >> 7, label & 127
+        pieces = []
+        for rest in values:
+            for _ in range(3):
+                rounded = rest.astype(jnp.bfloat16).astype(jnp.float32)
+                pieces.append(rounded)
+                rest = rest - rounded
+        total = jnp.zeros((len(pieces) * across, along), jnp.float32)
+        for r in range(0, 2 * GROUP, 2):
+
+            def flat(array):
+                return jnp.concatenate([array[r : r + 1], array[r + 1 : r + 2]], axis=1)
+
+            at_x = iota((across, 2 * along), 0) == flat(label_x)
+            left = jnp.concatenate([jnp.where(at_x, flat(piece), 0.0) for piece in pieces], axis=0)
+            right = jnp.where(iota((along, 2 * along), 0) == flat(label_y), 1.0, 0.0)
+            total = total + lax.dot_general(
+                left.astype(jnp.bfloat16),
+                right.astype(jnp.bfloat16),
+                (((1,), (1,)), ((), ())),
+                preferred_element_type=jnp.float32,
+            )
+        return [
+            total[24 * k : 24 * k + 8] + total[24 * k + 8 : 24 * k + 16] + total[24 * k + 16 : 24 * k + 24]
+            for k in range(len(values))
+        ]
+
+    def plane_there(d, e):
+        crosses = jnp.bool_(False)
+        if d == 1:
+            crosses = i == half - 1
+        if d == -1:
+            crosses = i == half
+        return there((d, e, 0)) & jnp.logical_not(crosses)
+
+    def plane_copy(number):
+        d, e = BESIDE[number]
+        if e == 0:
+            rows = pl.ds(4 if d == 1 else 0, 4)
+            source, target = plane.at[0, rows], plane_side.at[rows]
+        else:
+            source, target = plane_parcel, plane_packed.at[{0: 0, 1: 1, -1: 2}[d], 0 if e == 1 else 1]
+        return pltpu.make_async_remote_copy(
+            src_ref=source,
+            dst_ref=target,
+            send_sem=plane_send.at[number],
+            recv_sem=plane_recv.at[number],
+            device_id=device((d, e, 0)),
+            device_id_type=MESH,
+        )
+
+    @pl.when(surface)
     def _():
         for layer in range(n_gz):
             for k in range(half):
@@ -492,40 +635,74 @@
                 total = jnp.where(place == layer, moved, total)
             return total
 
-        label = gather(2).astype(jnp.int32) - 1
-        label_x, label_y = label >> 7, label & 127
-        pieces = []
-        for kind in range(2):
-            rest = gather(kind)
-            for _ in range(3):
-                rounded = rest.astype(jnp.bfloat16).astype(jnp.float32)
-                pieces.append(rounded)
-                rest = rest - rounded
-        total = jnp.zeros((6 * across, along), jnp.float32)
-        for r in range(0, 2 * GROUP, 2):
-
-            def flat(array):
-                return jnp.concatenate([array[r : r + 1], array[r + 1 : r + 2]], axis=1)
-
-            at_x = iota((across, 2 * along), 0) == flat(label_x)
-            left = jnp.concatenate(
-                [jnp.where(at_x, flat(piece), 0.0) for piece in pieces], axis=0
-            )
-            right = jnp.where(iota((along, 2 * along), 0) == flat(label_y), 1.0, 0.0)
-            total = total + lax.dot_general(
-                left.astype(jnp.bfloat16),
-                right.astype(jnp.bfloat16),
-                (((1,), (1,)), ((), ())),
-                preferred_element_type=jnp.float32,
-            )
-        for k in range(2):
-            part = total[24 * k : 24 * k + 24]
-            plane[k] = part[0:8] + part[8:16] + part[16:24]
+        sums = add_up(gather(2).astype(jnp.int32) - 1, [gather(0), gather(1)])
+        plane[0] = sums[0]
+        plane[1] = sums[1]
+
+    @pl.when(surface & on_border)
+    def _():
+        for layer in range(n_gz):
+            for place in range(half):
+
+                @pl.when((layer > 0) | (border != place))
+                def _(layer=layer, place=place):
+                    far_parcel(layer, place).wait_recv()
+
+        parts = [jnp.sum(heap_far[layer], axis=0) for layer in range(4)]
+        front = lane % 8 < 4
+        values, labels = [], []
+        for k in (0, 2):
+            values.append(jnp.where(front, parts[k], pltpu.roll(parts[k + 1], SLOTS, 1)))
+            labels.append(jnp.where(front, pltpu.roll(parts[k], along - SLOTS, 1), parts[k + 1]))
+        label = jnp.concatenate(labels, axis=0).astype(jnp.int32) - 1
+        [total] = add_up(label, [jnp.concatenate(values, axis=0)])
+        plane_far[...] = total
+
+        @pl.when(high == 0)
+        def _():
+            plane_side[0:4] = total[0:4]
+
+        @pl.when(high != 0)
+        def _():
+            plane_side[4:8] = total[4:8]
+
+    @pl.when(surface)
+    def _():
+        plane_parcel[...] = jnp.where(
+            lane < 8, pltpu.roll(plane[0], 4, 1), pltpu.roll(plane_far[...], 12, 1)
+        )
+        for number, (d, e) in enumerate(BESIDE):
+
+            @pl.when(plane_there(d, e))
+            def _(number=number):
+                plane_copy(number).start()
+
+    depart(1)
+    arrive(1)
+    unpack(1)
+
+    @pl.when(surface)
+    def _():
+        for number, (d, e) in enumerate(BESIDE):
+
+            @pl.when(plane_there(-d, -e))
+            def _(number=number):
+                plane_copy(number).wait_recv()
+
+        def pair(kind):
+            return jnp.where(lane % 8 < 4, plane_packed[kind, 0], plane_packed[kind, 1])
+
+        same = pair(0)
+        edge = pltpu.roll(same, along - 4, 1)
+        corner = pltpu.roll(jnp.where(sub < 4, pair(2), pair(1)), along - 4, 1) + pltpu.roll(
+            same, along - 12, 1
+        )
         for f in range(2):
             body[1, f, 4] = body[1, f, 4] + plane[0]
-
-    pack(1)
-    begin(1)
+            side[1, f, 4] = side[1, f, 4] + plane_side[...]
+            edge_y[f, 4] = edge_y[f, 4] + edge
+            edge_xy[f, 0] = edge_xy[f, 0] + corner
+
     stores = [
         pltpu.make_async_copy(body.at[1, 0, pl.ds(4, depth)], prior_p, store_sem.at[0]),
         pltpu.make_async_copy(body.at[1, 1, pl.ds(4, depth)], prior_q, store_sem.at[1]),
@@ -534,11 +711,9 @@
     ]
     stores[0].start()
     stores[1].start()
-    arrive(1)
-    unpack(1)
     advance(1, finish)
 
-    @pl.when(g == 0)
+    @pl.when(surface)
     def _():
         for f in range(2):
             result[f, 0] = result[f, 0] + plane[1]
@@ -546,19 +721,40 @@
     stores[2].start()
     stores[3].start()
     depart(0)
-    depart(1)
-    for k in range(1, ring):
-        letter(k).wait_send()
-    for k in range(half):
-        if k > 0:
-            parcel_of(k, g).wait_send()
-        else:
-
-            @pl.when(g > 0)
-            def _():
-                parcel_of(0, g).wait_send()
+    for k in range(-quarter, quarter):
+        if k != 0:
+            letter(k).wait_send()
+    for k in near_ring:
+        relay(k).wait_send()
+    for k in range(1, half):
+        parcel_of(k, g).wait_send()
+
+    @pl.when(jnp.logical_not(surface))
+    def _():
+        parcel_of(0, g).wait_send()
+
+    @pl.when(jnp.logical_not(surface & on_border))
+    def _():
+        far_parcel(g, low).wait_send()
+
+    @pl.when(surface)
+    def _():
+        for number, (d, e) in enumerate(BESIDE):
+
+            @pl.when(plane_there(d, e))
+            def _(number=number):
+                plane_copy(number).wait_send()
 
     for copy in stores:
+        copy.wait()
+
+
+def hand_over(*refs):
+    sources, targets, sem = refs[:4], refs[4:8], refs[8]
+    copies = [pltpu.make_async_copy(a, b, sem.at[k]) for k, (a, b) in enumerate(zip(sources, targets))]
+    for copy in copies:
+        copy.start()
+    for copy in copies:
         copy.wait()
 
 
@@ -569,7 +765,7 @@
     n_traces = samples.shape[0]
     receivers = [ids.reshape(1, -1) for ids in (row, column, line)]
     f32 = jnp.float32
-    return pl.pallas_call(
+    outs = pl.pallas_call(
         functools.partial(kernel, sizes),
         out_shape=[jax.ShapeDtypeStruct(block, f32)] * 4,
         in_specs=[pl.BlockSpec(memory_space=pltpu.HBM)] * 17,
@@ -588,26 +784,48 @@
             pltpu.VMEM(weights.shape, f32),
             pltpu.VMEM((1, gain.shape[0]), f32),
             pltpu.VMEM((3, 1, n_traces), jnp.int32),
-            pltpu.VMEM((RING, 128), f32),
-            pltpu.VMEM((RING, 128), f32),
+            pltpu.VMEM((2, RING, 128), f32),
+            pltpu.VMEM((2, RING, 128), f32),
+            pltpu.VMEM((2, RING, 128), f32),
             pltpu.VMEM((2, GROUP, 128), f32),
+            pltpu.VMEM((8, 128), f32),
             pltpu.VMEM((4, 2, GROUP, 128), f32),
+            pltpu.VMEM((4, GROUP, 8, 128), f32),
             pltpu.VMEM((2, 8, 128), f32),
+            pltpu.VMEM((8, 128), f32),
+            pltpu.VMEM((8, 128), f32),
+            pltpu.VMEM((8, 128), f32),
+            pltpu.VMEM((3, 2, 8, 128), f32),
             pltpu.VMEM((2, 8, 8, 128), f32),
             pltpu.SemaphoreType.DMA((17,)),
             pltpu.SemaphoreType.DMA((4,)),
             pltpu.SemaphoreType.DMA((2, len(OFFSETS))),
             pltpu.SemaphoreType.DMA((2, len(OFFSETS))),
-            pltpu.SemaphoreType.DMA((RING,)),
-            pltpu.SemaphoreType.DMA((RING,)),
+            pltpu.SemaphoreType.DMA((9,)),
+            pltpu.SemaphoreType.DMA((9,)),
+            pltpu.SemaphoreType.DMA((9,)),
+            pltpu.SemaphoreType.DMA((9,)),
             pltpu.SemaphoreType.DMA((GROUP,)),
             pltpu.SemaphoreType.DMA((4, GROUP)),
+            pltpu.SemaphoreType.DMA,
+            pltpu.SemaphoreType.DMA((4, GROUP)),
+            pltpu.SemaphoreType.DMA((8,)),
+            pltpu.SemaphoreType.DMA((8,)),
         ],
         compiler_params=pltpu.CompilerParams(
             collective_id=0, has_side_effects=True, vmem_limit_bytes=60 * 2**20
         ),
         name="wave_steps",
     )(*fields, samples, weights, gain.reshape(1, -1), *receivers)
+    return pl.pallas_call(
+        hand_over,
+        out_shape=[jax.ShapeDtypeStruct(block, f32)] * 4,
+        in_specs=[pl.BlockSpec(memory_space=pltpu.HBM)] * 4,
+        out_specs=[pl.BlockSpec(memory_space=pltpu.HBM)] * 4,
+        scratch_shapes=[pltpu.SemaphoreType.DMA((4,))],
+        compiler_params=pltpu.CompilerParams(vmem_limit_bytes=60 * 2**20),
+        name="hand_over",
+    )(*outs)
 
 
 def solution(mesh):

time: 47.3 us -> 45.2 us (0.956)
  the two profiles are of different devices: /device:TPU:59 before, /device:TPU:25 now
where the time goes in v2:
time: 45.2 us; the launch traced here: 44.6 us
  Pallas kernels  44 us (97%)
  between operations  0.65 us (1%)
    pallas_call x1, Pallas kernels, local(): pl.pallas_call(functools.partial(kernel, sizes), out_shape=[jax.ShapeDtyp...  38.8 us
    pallas_call x1, Pallas kernels, local(): pl.pallas_call(hand_over, out_shape=[jax.ShapeDtypeStruct(block, f32)] *...  5.11 us

profile of v2, /device:TPU:25, one launch (start us, length us, event | category | flops | bytes accessed | tf_op | source)
XLA Modules:
  0.0 44.6 jit_solution(2888272573501830768)
XLA Ops:
  0.6 38.8 %wave_steps.1 = (f32[8,8,128]{2,1,0:T(8,128)}, f32[8,8,128]{2,1,0:T(8,128)}, f32[8,8,128]{2,1,0:T(8,128)}, f32[8,8,128]{2,1,0:T(8,128)}) custom-call(f32[8,8,128]{2,1,0:T(8,128)} %refs_0_.1, f32[8,8,128]{2,1,0:T(8,128)} %refs_1_.1, f32[8,8,128]{2,1,0:T(8,128)} %refs_2_.1, f32[8,8,128]{2,1,0:T(8,128)} %refs_3_.1, f32[8,8,128]{2,1,0:T(8,128)} %refs_4_.1, ...), custom_call_target="tpu_custom_call" | custom-call | tf_op jit(solution)/shard_map/wave_steps/pallas_call | solution.py:768
  39.5 5.1 %hand_over.1 = (f32[8,8,128]{2,1,0:T(8,128)}, f32[8,8,128]{2,1,0:T(8,128)}, f32[8,8,128]{2,1,0:T(8,128)}, f32[8,8,128]{2,1,0:T(8,128)}) custom-call(f32[8,8,128]{2,1,0:T(8,128)} %get-tuple-element.8.refs_0_, f32[8,8,128]{2,1,0:T(8,128)} %get-tuple-element.9.refs_1_, f32[8,8,128]{2,1,0:T(8,128)} %get-tuple-element.10.refs_2_, ...), custom_call_target="tpu_custom_call" | custom-call | tf_op jit(solution)/shard_map/hand_over/pallas_call | solution.py:820

commit v3 on v2

--- a/solution.py
+++ b/solution.py
@@ -101,9 +101,7 @@
         plane_side,
         plane_parcel,
         plane_packed,
-        result,
         load_sem,
-        store_sem,
         send_sem,
         recv_sem,
         letter_send,
@@ -456,10 +454,10 @@
             heap_far[0, border] = bundle_far[...]
 
     pl.semaphore_wait(barrier, count)
-    begin(0)
     for k in range(-quarter, quarter):
         if k != 0:
             letter(k).start()
+    begin(0)
     own = pl.ds(2 * quarter, 2)
     transit[:, own] = letters[:, own]
     for k in range(-quarter, quarter):
@@ -547,8 +545,8 @@
         body[1, 1, z + 4] = new_q
 
     def finish(z, new_p, new_q):
-        result[0, z] = new_p
-        result[1, z] = new_q
+        next_p[z] = new_p
+        next_q[z] = new_q
 
     late = (high == 0) & on_border
 
@@ -703,23 +701,15 @@
             edge_y[f, 4] = edge_y[f, 4] + edge
             edge_xy[f, 0] = edge_xy[f, 0] + corner
 
-    stores = [
-        pltpu.make_async_copy(body.at[1, 0, pl.ds(4, depth)], prior_p, store_sem.at[0]),
-        pltpu.make_async_copy(body.at[1, 1, pl.ds(4, depth)], prior_q, store_sem.at[1]),
-        pltpu.make_async_copy(result.at[0], next_p, store_sem.at[2]),
-        pltpu.make_async_copy(result.at[1], next_q, store_sem.at[3]),
-    ]
-    stores[0].start()
-    stores[1].start()
+    for f, prior in enumerate((prior_p, prior_q)):
+        prior[...] = body[1, f, 4:12]
     advance(1, finish)
 
     @pl.when(surface)
     def _():
-        for f in range(2):
-            result[f, 0] = result[f, 0] + plane[1]
-
-    stores[2].start()
-    stores[3].start()
+        for result in (next_p, next_q):
+            result[0] = result[0] + plane[1]
+
     depart(0)
     for k in range(-quarter, quarter):
         if k != 0:
@@ -744,9 +734,6 @@
             @pl.when(plane_there(d, e))
             def _(number=number):
                 plane_copy(number).wait_send()
-
-    for copy in stores:
-        copy.wait()
 
 
 def hand_over(*refs):
@@ -767,9 +754,9 @@
     f32 = jnp.float32
     outs = pl.pallas_call(
         functools.partial(kernel, sizes),
-        out_shape=[jax.ShapeDtypeStruct(block, f32)] * 4,
+        out_shape=[pltpu.VMEM(block, f32)] * 4,
         in_specs=[pl.BlockSpec(memory_space=pltpu.HBM)] * 17,
-        out_specs=[pl.BlockSpec(memory_space=pltpu.HBM)] * 4,
+        out_specs=[pl.BlockSpec(memory_space=pltpu.VMEM)] * 4,
         scratch_shapes=[
             pltpu.VMEM((2, 2, 16, 8, 128), f32),
             pltpu.VMEM((2, 2, 16, 8, 128), f32),
@@ -796,9 +783,7 @@
             pltpu.VMEM((8, 128), f32),
             pltpu.VMEM((8, 128), f32),
             pltpu.VMEM((3, 2, 8, 128), f32),
-            pltpu.VMEM((2, 8, 8, 128), f32),
             pltpu.SemaphoreType.DMA((17,)),
-            pltpu.SemaphoreType.DMA((4,)),
             pltpu.SemaphoreType.DMA((2, len(OFFSETS))),
             pltpu.SemaphoreType.DMA((2, len(OFFSETS))),
             pltpu.SemaphoreType.DMA((9,)),
@@ -820,10 +805,10 @@
     return pl.pallas_call(
         hand_over,
         out_shape=[jax.ShapeDtypeStruct(block, f32)] * 4,
-        in_specs=[pl.BlockSpec(memory_space=pltpu.HBM)] * 4,
+        in_specs=[pl.BlockSpec(memory_space=pl.ANY)] * 4,
         out_specs=[pl.BlockSpec(memory_space=pltpu.HBM)] * 4,
         scratch_shapes=[pltpu.SemaphoreType.DMA((4,))],
-        compiler_params=pltpu.CompilerParams(vmem_limit_bytes=60 * 2**20),
+        compiler_params=pltpu.CompilerParams(vmem_limit_bytes=2**20),
         name="hand_over",
     )(*outs)
 

time: 45.2 us -> 39.7 us (0.88); the launches traced: 44.6 us -> 39.6 us
  Pallas kernels: 44 us -> 38.9 us
    pallas_call x1, Pallas kernels: 5.11 us -> 0.69 us  [local(): pl.pallas_call(hand_over, out_shape=[jax.ShapeDtypeStruct(block, f32)] *...]
    pallas_call x1, Pallas kernels: 38.8 us -> 38.3 us  [local(): pl.pallas_call(functools.partial(kernel, sizes), out_shape=[pltpu.VMEM(bl...]
where the time goes in v3:
time: 39.7 us; the launch traced here: 39.6 us
  Pallas kernels  38.9 us (98%)
  between operations  0.65 us (2%)
    pallas_call x1, Pallas kernels, local(): pl.pallas_call(functools.partial(kernel, sizes), out_shape=[pltpu.VMEM(bl...  38.3 us

profile of v3, /device:TPU:25, one launch (start us, length us, event | category | flops | bytes accessed | tf_op | source)
XLA Modules:
  0.0 39.6 jit_solution(3139746910124023223)
XLA Ops:
  0.6 38.3 %wave_steps.1 = (f32[8,8,128]{2,1,0:T(8,128)S(1)}, f32[8,8,128]{2,1,0:T(8,128)S(1)}, f32[8,8,128]{2,1,0:T(8,128)S(1)}, f32[8,8,128]{2,1,0:T(8,128)S(1)}) custom-call(f32[8,8,128]{2,1,0:T(8,128)} %refs_0_.1, f32[8,8,128]{2,1,0:T(8,128)} %refs_1_.1, f32[8,8,128]{2,1,0:T(8,128)} %refs_2_.1, f32[8,8,128]{2,1,0:T(8,128)} %refs_3_.1, f32[8,8,128]{2,1,0:T(8,128)} %refs_4_.1, ...), custom_call_target="tpu_custom_call" | custom-call | tf_op jit(solution)/shard_map/wave_steps/pallas_call | solution.py:755
  38.9 0.7 %hand_over.1 = (f32[8,8,128]{2,1,0:T(8,128)}, f32[8,8,128]{2,1,0:T(8,128)}, f32[8,8,128]{2,1,0:T(8,128)}, f32[8,8,128]{2,1,0:T(8,128)}) custom-call(f32[8,8,128]{2,1,0:T(8,128)S(1)} %get-tuple-element.8.refs_0_, f32[8,8,128]{2,1,0:T(8,128)S(1)} %get-tuple-element.9.refs_1_, f32[8,8,128]{2,1,0:T(8,128)S(1)} %get-tuple-element.10.refs_2_, ...), custom_call_target="tpu_custom_call" | custom-call | tf_op jit(solution)/shard_map/hand_over/pallas_call | solution.py:805

commit v4 on v3

--- a/solution.py
+++ b/solution.py
@@ -92,6 +92,8 @@
         letters,
         transit,
         mail,
+        passing,
+        passing_parcel,
         bundle,
         bundle_far,
         heap,
@@ -114,6 +116,10 @@
         far_recv,
         plane_send,
         plane_recv,
+        pass_send,
+        pass_recv,
+        onward_send,
+        known,
     ) = refs
     i = lax.axis_index("inl")
     j = lax.axis_index("xl")
@@ -127,6 +133,8 @@
     border = jnp.where(high == 0, half - 1, 0)
     on_border = low == border
     surface = g == 0
+    near_side, far_side = i == half - 1, i == half
+    forwards = (low == half - 1) & (level >= quarter) & (level < quarter + n_xl)
 
     loads = [
         (wave_p, body.at[0, 0, pl.ds(4, depth)]),
@@ -148,9 +156,6 @@
         (shot, small_r.at[2]),
     ]
     loads = [pltpu.make_async_copy(a, b, load_sem.at[k]) for k, (a, b) in enumerate(loads)]
-    for copy in loads:
-        copy.start()
-
     nothing = jnp.zeros((2, 4, across, along), jnp.float32)
     for turn in range(2):
         body[turn, :, 0:4] = nothing
@@ -193,16 +198,47 @@
 
     barrier = pltpu.get_barrier_semaphore()
     count = jnp.int32(2 * quarter) + jnp.where(surface, half - 1, half)
-    for offset in OFFSETS:
-
-        @pl.when(there(offset))
-        def _(offset=offset):
-            pl.semaphore_signal(barrier, inc=1, device_id=device(offset), device_id_type=MESH)
-
-        count = count + there(offset).astype(jnp.int32)
     near_ring = [k for k in range(-quarter, quarter + 1) if k != 0]
     for k in near_ring:
         pl.semaphore_signal(barrier, inc=1, device_id=on_ring(k), device_id_type=MESH)
+
+    def inside(place, count):
+        return (place >= 0) & (place < count)
+
+    def from_half_way(offset):
+        _, e, f = offset
+        ok = far_side & inside(j - e, n_xl) & inside(g - f, n_gz)
+        place = jnp.clip(j - e, 0, n_xl - 1) + quarter
+        return ok, (place // n_xl * half + half - 1, lax.rem(place, n_xl), jnp.clip(g - f, 0, n_gz - 1))
+
+    def to_far_side(offset):
+        _, e, f = offset
+        place = level - quarter + e
+        ok = forwards & inside(place, n_xl) & inside(g + f, n_gz)
+        return ok, (half, jnp.clip(place, 0, n_xl - 1), jnp.clip(g + f, 0, n_gz - 1))
+
+    for offset in OFFSETS:
+        d = offset[0]
+        hears = there(offset)
+        if d == -1:
+            hears = hears & jnp.logical_not(far_side)
+        if d == 1:
+            ok, whom = from_half_way(offset)
+
+            @pl.when(ok)
+            def _(whom=whom):
+                pl.semaphore_signal(barrier, inc=1, device_id=whom, device_id_type=MESH)
+
+            count = count + to_far_side(offset)[0].astype(jnp.int32)
+
+        @pl.when(hears)
+        def _(offset=offset):
+            pl.semaphore_signal(barrier, inc=1, device_id=device(offset), device_id_type=MESH)
+
+        direct = there(offset)
+        if d == 1:
+            direct = direct & jnp.logical_not(near_side)
+        count = count + direct.astype(jnp.int32)
 
     @pl.when(surface)
     def _():
@@ -213,6 +249,8 @@
                         barrier, inc=1, device_id=in_group(k, layer), device_id_type=MESH
                     )
 
+    for copy in loads:
+        copy.start()
     for copy in loads:
         copy.wait()
 
@@ -355,10 +393,15 @@
             )
         return out
 
+    def sends(turn, offset):
+        if turn == 0 and offset[0] == 1:
+            return there(offset) & jnp.logical_not(near_side)
+        return there(offset)
+
     def begin(turn):
         for offset, copy in zip(OFFSETS, copies(turn)):
 
-            @pl.when(there(offset))
+            @pl.when(sends(turn, offset))
             def _(copy=copy):
                 copy.start()
 
@@ -372,9 +415,40 @@
     def depart(turn):
         for offset, copy in zip(OFFSETS, copies(turn)):
 
-            @pl.when(there(offset))
+            @pl.when(sends(turn, offset))
             def _(copy=copy):
                 copy.wait_send()
+
+    def to_half_way(part):
+        source = body.at[0, :, pl.ds(4, depth), pl.ds(4, 4)] if part == 0 else parcel.at[0]
+        return pltpu.make_async_remote_copy(
+            src_ref=source,
+            dst_ref=passing if part == 0 else passing_parcel,
+            send_sem=pass_send.at[part],
+            recv_sem=pass_recv.at[part],
+            device_id=on_ring(quarter),
+            device_id_type=MESH,
+        )
+
+    def onward(number):
+        _, e, f = OFFSETS[number]
+        if e != 0:
+            source = passing_parcel
+            target = packed.at[0, 3, 0 if e == 1 else 1]
+        else:
+            first, deep, goal = {0: (0, 8, 4), 1: (4, 4, 0), -1: (0, 4, 12)}[f]
+            source = passing.at[:, pl.ds(first, deep)]
+            target = side.at[0, :, pl.ds(goal, deep), pl.ds(4, 4)]
+        return pltpu.make_async_remote_copy(
+            src_ref=source,
+            dst_ref=target,
+            send_sem=onward_send.at[number],
+            recv_sem=recv_sem.at[0, number],
+            device_id=to_far_side(OFFSETS[number])[1],
+            device_id_type=MESH,
+        )
+
+    crossing = [number for number, offset in enumerate(OFFSETS) if offset[0] == 1]
 
     def letter(k):
         rows = pl.ds(2 * (k + quarter), 2)
@@ -457,7 +531,25 @@
     for k in range(-quarter, quarter):
         if k != 0:
             letter(k).start()
+
+    @pl.when(near_side)
+    def _():
+        for part in range(2):
+            to_half_way(part).start()
+
     begin(0)
+
+    @pl.when(forwards)
+    def _():
+        pl.semaphore_signal(known, inc=1, device_id=on_ring(-quarter), device_id_type=MESH)
+        for part in range(2):
+            to_half_way(part).wait_recv()
+        for number in crossing:
+
+            @pl.when(to_far_side(OFFSETS[number])[0])
+            def _(number=number):
+                onward(number).start()
+
     own = pl.ds(2 * quarter, 2)
     transit[:, own] = letters[:, own]
     for k in range(-quarter, quarter):
@@ -558,6 +650,11 @@
     unpack(0)
     advance(0, keep)
     pack(1)
+
+    @pl.when(near_side)
+    def _():
+        pl.semaphore_wait(known, 1)
+
     begin(1)
 
     @pl.when(jnp.logical_not(late))
@@ -711,6 +808,20 @@
             result[0] = result[0] + plane[1]
 
     depart(0)
+
+    @pl.when(near_side)
+    def _():
+        for part in range(2):
+            to_half_way(part).wait_send()
+
+    @pl.when(forwards)
+    def _():
+        for number in crossing:
+
+            @pl.when(to_far_side(OFFSETS[number])[0])
+            def _(number=number):
+                onward(number).wait_send()
+
     for k in range(-quarter, quarter):
         if k != 0:
             letter(k).wait_send()
@@ -774,6 +885,8 @@
             pltpu.VMEM((2, RING, 128), f32),
             pltpu.VMEM((2, RING, 128), f32),
             pltpu.VMEM((2, RING, 128), f32),
+            pltpu.VMEM((2, 8, 4, 128), f32),
+            pltpu.VMEM((8, 128), f32),
             pltpu.VMEM((2, GROUP, 128), f32),
             pltpu.VMEM((8, 128), f32),
             pltpu.VMEM((4, 2, GROUP, 128), f32),
@@ -796,6 +909,10 @@
             pltpu.SemaphoreType.DMA((4, GROUP)),
             pltpu.SemaphoreType.DMA((8,)),
             pltpu.SemaphoreType.DMA((8,)),
+            pltpu.SemaphoreType.DMA((2,)),
+            pltpu.SemaphoreType.DMA((2,)),
+            pltpu.SemaphoreType.DMA((len(OFFSETS),)),
+            pltpu.SemaphoreType.REGULAR,
         ],
         compiler_params=pltpu.CompilerParams(
             collective_id=0, has_side_effects=True, vmem_limit_bytes=60 * 2**20

time: 39.7 us -> 38.6 us (0.972); the launches traced: 39.6 us -> 38.1 us
  Pallas kernels: 38.9 us -> 37.4 us
    pallas_call x1, Pallas kernels: 38.3 us -> 36.7 us  [local(): pl.pallas_call(functools.partial(kernel, sizes), out_shape=[pltpu.VMEM(bl...]
where the time goes in v4:
time: 38.6 us; the launch traced here: 38.1 us
  Pallas kernels  37.4 us (97%)
  between operations  0.65 us (2%)
    pallas_call x1, Pallas kernels, local(): pl.pallas_call(functools.partial(kernel, sizes), out_shape=[pltpu.VMEM(bl...  36.7 us

profile of v4, /device:TPU:25, one launch (start us, length us, event | category | flops | bytes accessed | tf_op | source)
XLA Modules:
  0.0 38.1 jit_solution(9132443544134580302)
XLA Ops:
  0.6 36.7 %wave_steps.1 = (f32[8,8,128]{2,1,0:T(8,128)S(1)}, f32[8,8,128]{2,1,0:T(8,128)S(1)}, f32[8,8,128]{2,1,0:T(8,128)S(1)}, f32[8,8,128]{2,1,0:T(8,128)S(1)}) custom-call(f32[8,8,128]{2,1,0:T(8,128)} %refs_0_.1, f32[8,8,128]{2,1,0:T(8,128)} %refs_1_.1, f32[8,8,128]{2,1,0:T(8,128)} %refs_2_.1, f32[8,8,128]{2,1,0:T(8,128)} %refs_3_.1, f32[8,8,128]{2,1,0:T(8,128)} %refs_4_.1, ...), custom_call_target="tpu_custom_call" | custom-call | tf_op jit(solution)/shard_map/wave_steps/pallas_call | solution.py:866
  37.4 0.7 %hand_over.1 = (f32[8,8,128]{2,1,0:T(8,128)}, f32[8,8,128]{2,1,0:T(8,128)}, f32[8,8,128]{2,1,0:T(8,128)}, f32[8,8,128]{2,1,0:T(8,128)}) custom-call(f32[8,8,128]{2,1,0:T(8,128)S(1)} %get-tuple-element.8.refs_0_, f32[8,8,128]{2,1,0:T(8,128)S(1)} %get-tuple-element.9.refs_1_, f32[8,8,128]{2,1,0:T(8,128)S(1)} %get-tuple-element.10.refs_2_, ...), custom_call_target="tpu_custom_call" | custom-call | tf_op jit(solution)/shard_map/hand_over/pallas_call | solution.py:922

commit v5 on v4

--- a/solution.py
+++ b/solution.py
@@ -630,7 +630,7 @@
             store(z, new_p, new_q)
             return 0
 
-        lax.fori_loop(0, depth, layer, 0)
+        lax.fori_loop(0, depth, layer, 0, unroll=8)
 
     def keep(z, new_p, new_q):
         body[1, 0, z + 4] = new_p

time: 38.6 us -> 38.1 us (0.987)
  the two profiles are of different devices: /device:TPU:25 before, /device:TPU:1 now
where the time goes in v5:
time: 38.1 us; the launch traced here: 38 us
  Pallas kernels  37.3 us (98%)
  between operations  0.65 us (2%)
    pallas_call x1, Pallas kernels, local(): pl.pallas_call(functools.partial(kernel, sizes), out_shape=[pltpu.VMEM(bl...  36.6 us

profile of v5, /device:TPU:1, one launch (start us, length us, event | category | flops | bytes accessed | tf_op | source)
XLA Modules:
  0.0 38.0 jit_solution(7580647262277461892)
XLA Ops:
  0.6 36.6 %wave_steps.1 = (f32[8,8,128]{2,1,0:T(8,128)S(1)}, f32[8,8,128]{2,1,0:T(8,128)S(1)}, f32[8,8,128]{2,1,0:T(8,128)S(1)}, f32[8,8,128]{2,1,0:T(8,128)S(1)}) custom-call(f32[8,8,128]{2,1,0:T(8,128)} %refs_0_.1, f32[8,8,128]{2,1,0:T(8,128)} %refs_1_.1, f32[8,8,128]{2,1,0:T(8,128)} %refs_2_.1, f32[8,8,128]{2,1,0:T(8,128)} %refs_3_.1, f32[8,8,128]{2,1,0:T(8,128)} %refs_4_.1, ...), custom_call_target="tpu_custom_call" | custom-call | tf_op jit(solution)/shard_map/wave_steps/pallas_call | solution.py:866
  37.3 0.7 %hand_over.1 = (f32[8,8,128]{2,1,0:T(8,128)}, f32[8,8,128]{2,1,0:T(8,128)}, f32[8,8,128]{2,1,0:T(8,128)}, f32[8,8,128]{2,1,0:T(8,128)}) custom-call(f32[8,8,128]{2,1,0:T(8,128)S(1)} %get-tuple-element.8.refs_0_, f32[8,8,128]{2,1,0:T(8,128)S(1)} %get-tuple-element.9.refs_1_, f32[8,8,128]{2,1,0:T(8,128)S(1)} %get-tuple-element.10.refs_2_, ...), custom_call_target="tpu_custom_call" | custom-call | tf_op jit(solution)/shard_map/hand_over/pallas_call | solution.py:922

commit v6 on v5

--- a/solution.py
+++ b/solution.py
@@ -120,6 +120,8 @@
         pass_recv,
         onward_send,
         known,
+        direct_send,
+        direct_recv,
     ) = refs
     i = lax.axis_index("inl")
     j = lax.axis_index("xl")
@@ -133,6 +135,7 @@
     border = jnp.where(high == 0, half - 1, 0)
     on_border = low == border
     surface = g == 0
+    even, odd = low % 2 == 0, low % 2 == 1
     near_side, far_side = i == half - 1, i == half
     forwards = (low == half - 1) & (level >= quarter) & (level < quarter + n_xl)
 
@@ -197,10 +200,19 @@
         return (high * half + lax.rem(low + k, half), j, layer)
 
     barrier = pltpu.get_barrier_semaphore()
-    count = jnp.int32(2 * quarter) + jnp.where(surface, half - 1, half)
+    count = jnp.where(even, ring - 1, 2 * quarter) + jnp.where(surface, half - 1, half)
     near_ring = [k for k in range(-quarter, quarter + 1) if k != 0]
-    for k in near_ring:
-        pl.semaphore_signal(barrier, inc=1, device_id=on_ring(k), device_id_type=MESH)
+    far_ring = [k for k in range(-ring // 2, ring // 2) if k != 0]
+
+    @pl.when(even)
+    def _():
+        for k in far_ring:
+            pl.semaphore_signal(barrier, inc=1, device_id=on_ring(k), device_id_type=MESH)
+
+    @pl.when(odd)
+    def _():
+        for k in near_ring:
+            pl.semaphore_signal(barrier, inc=1, device_id=on_ring(k), device_id_type=MESH)
 
     def inside(place, count):
         return (place >= 0) & (place < count)
@@ -461,6 +473,17 @@
             device_id_type=MESH,
         )
 
+    def direct_letter(k):
+        row = pl.ds(k + ring // 2, 1)
+        return pltpu.make_async_remote_copy(
+            src_ref=letters.at[:, row],
+            dst_ref=mail.at[:, row],
+            send_sem=direct_send.at[k + ring // 2],
+            recv_sem=direct_recv.at[k + ring // 2],
+            device_id=on_ring(k),
+            device_id_type=MESH,
+        )
+
     def relay_rows(k):
         first = max(2 * (k + quarter) - 1, 0)
         return first, min(2 * (k + quarter) + 1, ring) - first
@@ -497,8 +520,16 @@
         )
 
     def post():
-        for k in near_ring:
-            relay(k).wait_recv()
+        @pl.when(even)
+        def _():
+            for k in far_ring:
+                direct_letter(k).wait_recv()
+
+        @pl.when(odd)
+        def _():
+            for k in near_ring:
+                relay(k).wait_recv()
+
         for t in range(2):
             got = mail[0, 8 * t : 8 * t + 8, :]
             turned = jnp.zeros((GROUP, along), jnp.float32)
@@ -528,9 +559,17 @@
             heap_far[0, border] = bundle_far[...]
 
     pl.semaphore_wait(barrier, count)
-    for k in range(-quarter, quarter):
-        if k != 0:
-            letter(k).start()
+
+    @pl.when(even)
+    def _():
+        for k in far_ring:
+            direct_letter(k).start()
+
+    @pl.when(odd)
+    def _():
+        for k in range(-quarter, quarter):
+            if k != 0:
+                letter(k).start()
 
     @pl.when(near_side)
     def _():
@@ -550,15 +589,22 @@
             def _(number=number):
                 onward(number).start()
 
-    own = pl.ds(2 * quarter, 2)
-    transit[:, own] = letters[:, own]
-    for k in range(-quarter, quarter):
-        if k != 0:
-            letter(k).wait_recv()
-    for k in near_ring:
-        relay(k).start()
-    kept = pl.ds(*relay_rows(0))
-    mail[:, kept] = transit[:, kept]
+    @pl.when(even)
+    def _():
+        own = pl.ds(ring // 2, 1)
+        mail[:, own] = letters[:, own]
+
+    @pl.when(odd)
+    def _():
+        own = pl.ds(2 * quarter, 2)
+        transit[:, own] = letters[:, own]
+        for k in range(-quarter, quarter):
+            if k != 0:
+                letter(k).wait_recv()
+        for k in near_ring:
+            relay(k).start()
+        kept = pl.ds(*relay_rows(0))
+        mail[:, kept] = transit[:, kept]
 
     def unpack(turn):
         def pair(kind):
@@ -713,6 +759,14 @@
             device_id_type=MESH,
         )
 
+    def plane_start(parcels):
+        for number, (d, e) in enumerate(BESIDE):
+            if (e != 0) == parcels:
+
+                @pl.when(plane_there(d, e))
+                def _(number=number):
+                    plane_copy(number).start()
+
     @pl.when(surface)
     def _():
         for layer in range(n_gz):
@@ -733,6 +787,7 @@
         sums = add_up(gather(2).astype(jnp.int32) - 1, [gather(0), gather(1)])
         plane[0] = sums[0]
         plane[1] = sums[1]
+        plane_start(False)
 
     @pl.when(surface & on_border)
     def _():
@@ -766,11 +821,7 @@
         plane_parcel[...] = jnp.where(
             lane < 8, pltpu.roll(plane[0], 4, 1), pltpu.roll(plane_far[...], 12, 1)
         )
-        for number, (d, e) in enumerate(BESIDE):
-
-            @pl.when(plane_there(d, e))
-            def _(number=number):
-                plane_copy(number).start()
+        plane_start(True)
 
     depart(1)
     arrive(1)
@@ -822,11 +873,19 @@
             def _(number=number):
                 onward(number).wait_send()
 
-    for k in range(-quarter, quarter):
-        if k != 0:
-            letter(k).wait_send()
-    for k in near_ring:
-        relay(k).wait_send()
+    @pl.when(even)
+    def _():
+        for k in far_ring:
+            direct_letter(k).wait_send()
+
+    @pl.when(odd)
+    def _():
+        for k in range(-quarter, quarter):
+            if k != 0:
+                letter(k).wait_send()
+        for k in near_ring:
+            relay(k).wait_send()
+
     for k in range(1, half):
         parcel_of(k, g).wait_send()
 
@@ -913,6 +972,8 @@
             pltpu.SemaphoreType.DMA((2,)),
             pltpu.SemaphoreType.DMA((len(OFFSETS),)),
             pltpu.SemaphoreType.REGULAR,
+            pltpu.SemaphoreType.DMA((RING,)),
+            pltpu.SemaphoreType.DMA((RING,)),
         ],
         compiler_params=pltpu.CompilerParams(
             collective_id=0, has_side_effects=True, vmem_limit_bytes=60 * 2**20

time: 38.1 us -> 37.4 us (0.982)
  the two profiles are of different devices: /device:TPU:1 before, /device:TPU:25 now
where the time goes in v6:
time: 37.4 us; the launch traced here: 37.2 us
  Pallas kernels  36.6 us (98%)
  between operations  0.65 us (2%)
    pallas_call x1, Pallas kernels, local(): pl.pallas_call(functools.partial(kernel, sizes), out_shape=[pltpu.VMEM(bl...  35.9 us

profile of v6, /device:TPU:25, one launch (start us, length us, event | category | flops | bytes accessed | tf_op | source)
XLA Modules:
  0.0 37.2 jit_solution(16480835707525134399)
XLA Ops:
  0.6 35.9 %wave_steps.1 = (f32[8,8,128]{2,1,0:T(8,128)S(1)}, f32[8,8,128]{2,1,0:T(8,128)S(1)}, f32[8,8,128]{2,1,0:T(8,128)S(1)}, f32[8,8,128]{2,1,0:T(8,128)S(1)}) custom-call(f32[8,8,128]{2,1,0:T(8,128)} %refs_0_.1, f32[8,8,128]{2,1,0:T(8,128)} %refs_1_.1, f32[8,8,128]{2,1,0:T(8,128)} %refs_2_.1, f32[8,8,128]{2,1,0:T(8,128)} %refs_3_.1, f32[8,8,128]{2,1,0:T(8,128)} %refs_4_.1, ...), custom_call_target="tpu_custom_call" | custom-call | tf_op jit(solution)/shard_map/wave_steps/pallas_call | solution.py:925
  36.5 0.7 %hand_over.1 = (f32[8,8,128]{2,1,0:T(8,128)}, f32[8,8,128]{2,1,0:T(8,128)}, f32[8,8,128]{2,1,0:T(8,128)}, f32[8,8,128]{2,1,0:T(8,128)}) custom-call(f32[8,8,128]{2,1,0:T(8,128)S(1)} %get-tuple-element.8.refs_0_, f32[8,8,128]{2,1,0:T(8,128)S(1)} %get-tuple-element.9.refs_1_, f32[8,8,128]{2,1,0:T(8,128)S(1)} %get-tuple-element.10.refs_2_, ...), custom_call_target="tpu_custom_call" | custom-call | tf_op jit(solution)/shard_map/hand_over/pallas_call | solution.py:983

commit v7 on v6

--- a/solution.py
+++ b/solution.py
@@ -12,9 +12,7 @@
 first_coef = (0.0, 4.0 / 5.0, -1.0 / 5.0, 4.0 / 105.0, -1.0 / 280.0)
 
 OFFSETS = (
-    [(d, 0, 0) for d in (1, -1)]
-    + [(d, 0, e) for d in (1, -1) for e in (1, -1)]
-    + [(d, e, 0) for d in (1, -1) for e in (1, -1)]
+    [(d, e, f) for d in (-1, 1) for e, f in ((0, 0), (0, 1), (0, -1), (1, 0), (-1, 0))]
     + [(0, d, e) for d in (1, -1) for e in (1, -1)]
     + [(0, d, 0) for d in (1, -1)]
     + [(0, 0, d) for d in (1, -1)]
@@ -418,7 +416,7 @@
                 copy.start()
 
     def arrive(turn):
-        for offset, copy in zip(OFFSETS, copies(turn)):
+        for offset, copy in list(zip(OFFSETS, copies(turn)))[::-1]:
 
             @pl.when(there(tuple(-d for d in offset)))
             def _(copy=copy):
@@ -824,8 +822,52 @@
         plane_start(True)
 
     depart(1)
-    arrive(1)
-    unpack(1)
+    depart(0)
+
+    @pl.when(near_side)
+    def _():
+        for part in range(2):
+            to_half_way(part).wait_send()
+
+    @pl.when(forwards)
+    def _():
+        for number in crossing:
+
+            @pl.when(to_far_side(OFFSETS[number])[0])
+            def _(number=number):
+                onward(number).wait_send()
+
+    @pl.when(even)
+    def _():
+        for k in far_ring:
+            direct_letter(k).wait_send()
+
+    @pl.when(odd)
+    def _():
+        for k in range(-quarter, quarter):
+            if k != 0:
+                letter(k).wait_send()
+        for k in near_ring:
+            relay(k).wait_send()
+
+    for k in range(1, half):
+        parcel_of(k, g).wait_send()
+
+    @pl.when(jnp.logical_not(surface))
+    def _():
+        parcel_of(0, g).wait_send()
+
+    @pl.when(jnp.logical_not(surface & on_border))
+    def _():
+        far_parcel(g, low).wait_send()
+
+    @pl.when(surface)
+    def _():
+        for number, (d, e) in enumerate(BESIDE):
+
+            @pl.when(plane_there(d, e))
+            def _(number=number):
+                plane_copy(number).wait_send()
 
     @pl.when(surface)
     def _():
@@ -835,6 +877,11 @@
             def _(number=number):
                 plane_copy(number).wait_recv()
 
+    arrive(1)
+    unpack(1)
+
+    @pl.when(surface)
+    def _():
         def pair(kind):
             return jnp.where(lane % 8 < 4, plane_packed[kind, 0], plane_packed[kind, 1])
 
@@ -857,53 +904,6 @@
     def _():
         for result in (next_p, next_q):
             result[0] = result[0] + plane[1]
-
-    depart(0)
-
-    @pl.when(near_side)
-    def _():
-        for part in range(2):
-            to_half_way(part).wait_send()
-
-    @pl.when(forwards)
-    def _():
-        for number in crossing:
-
-            @pl.when(to_far_side(OFFSETS[number])[0])
-            def _(number=number):
-                onward(number).wait_send()
-
-    @pl.when(even)
-    def _():
-        for k in far_ring:
-            direct_letter(k).wait_send()
-
-    @pl.when(odd)
-    def _():
-        for k in range(-quarter, quarter):
-            if k != 0:
-                letter(k).wait_send()
-        for k in near_ring:
-            relay(k).wait_send()
-
-    for k in range(1, half):
-        parcel_of(k, g).wait_send()
-
-    @pl.when(jnp.logical_not(surface))
-    def _():
-        parcel_of(0, g).wait_send()
-
-    @pl.when(jnp.logical_not(surface & on_border))
-    def _():
-        far_parcel(g, low).wait_send()
-
-    @pl.when(surface)
-    def _():
-        for number, (d, e) in enumerate(BESIDE):
-
-            @pl.when(plane_there(d, e))
-            def _(number=number):
-                plane_copy(number).wait_send()
 
 
 def hand_over(*refs):

time: 37.4 us -> 37.1 us (level)
  no operation moved by 1% of the time
where the time goes in v7:
time: 37.1 us; the launch traced here: 37 us
  Pallas kernels  36.3 us (98%)
  between operations  0.65 us (2%)
    pallas_call x1, Pallas kernels, local(): pl.pallas_call(functools.partial(kernel, sizes), out_shape=[pltpu.VMEM(bl...  35.6 us

profile of v7, /device:TPU:25, one launch (start us, length us, event | category | flops | bytes accessed | tf_op | source)
XLA Modules:
  0.0 37.0 jit_solution(1222649234878994432)
XLA Ops:
  0.6 35.6 %wave_steps.1 = (f32[8,8,128]{2,1,0:T(8,128)S(1)}, f32[8,8,128]{2,1,0:T(8,128)S(1)}, f32[8,8,128]{2,1,0:T(8,128)S(1)}, f32[8,8,128]{2,1,0:T(8,128)S(1)}) custom-call(f32[8,8,128]{2,1,0:T(8,128)} %refs_0_.1, f32[8,8,128]{2,1,0:T(8,128)} %refs_1_.1, f32[8,8,128]{2,1,0:T(8,128)} %refs_2_.1, f32[8,8,128]{2,1,0:T(8,128)} %refs_3_.1, f32[8,8,128]{2,1,0:T(8,128)} %refs_4_.1, ...), custom_call_target="tpu_custom_call" | custom-call | tf_op jit(solution)/shard_map/wave_steps/pallas_call | solution.py:925
  36.3 0.7 %hand_over.1 = (f32[8,8,128]{2,1,0:T(8,128)}, f32[8,8,128]{2,1,0:T(8,128)}, f32[8,8,128]{2,1,0:T(8,128)}, f32[8,8,128]{2,1,0:T(8,128)}) custom-call(f32[8,8,128]{2,1,0:T(8,128)S(1)} %get-tuple-element.8.refs_0_, f32[8,8,128]{2,1,0:T(8,128)S(1)} %get-tuple-element.9.refs_1_, f32[8,8,128]{2,1,0:T(8,128)S(1)} %get-tuple-element.10.refs_2_, ...), custom_call_target="tpu_custom_call" | custom-call | tf_op jit(solution)/shard_map/hand_over/pallas_call | solution.py:983

commit v8 on v7

--- a/solution.py
+++ b/solution.py
@@ -408,12 +408,13 @@
             return there(offset) & jnp.logical_not(near_side)
         return there(offset)
 
-    def begin(turn):
+    def begin(turn, packed_cells):
         for offset, copy in zip(OFFSETS, copies(turn)):
-
-            @pl.when(sends(turn, offset))
-            def _(copy=copy):
-                copy.start()
+            if (offset[1] != 0) == packed_cells:
+
+                @pl.when(sends(turn, offset))
+                def _(copy=copy):
+                    copy.start()
 
     def arrive(turn):
         for offset, copy in list(zip(OFFSETS, copies(turn)))[::-1]:
@@ -574,18 +575,20 @@
         for part in range(2):
             to_half_way(part).start()
 
-    begin(0)
+    begin(0, False)
+    begin(0, True)
 
     @pl.when(forwards)
     def _():
         pl.semaphore_signal(known, inc=1, device_id=on_ring(-quarter), device_id_type=MESH)
         for part in range(2):
             to_half_way(part).wait_recv()
-        for number in crossing:
-
-            @pl.when(to_far_side(OFFSETS[number])[0])
-            def _(number=number):
-                onward(number).start()
+            for number in crossing:
+                if (OFFSETS[number][1] != 0) == (part == 1):
+
+                    @pl.when(to_far_side(OFFSETS[number])[0])
+                    def _(number=number):
+                        onward(number).start()
 
     @pl.when(even)
     def _():
@@ -693,13 +696,14 @@
     arrive(0)
     unpack(0)
     advance(0, keep)
+
+    @pl.when(near_side)
+    def _():
+        pl.semaphore_wait(known, 1)
+
+    begin(1, False)
     pack(1)
-
-    @pl.when(near_side)
-    def _():
-        pl.semaphore_wait(known, 1)
-
-    begin(1)
+    begin(1, True)
 
     @pl.when(jnp.logical_not(late))
     def _():

time: 37.1 us -> 37 us (level)
  no operation moved by 1% of the time
where the time goes in v8:
time: 37 us; the launch traced here: 36.9 us
  Pallas kernels  36.2 us (98%)
  between operations  0.65 us (2%)
    pallas_call x1, Pallas kernels, local(): pl.pallas_call(functools.partial(kernel, sizes), out_shape=[pltpu.VMEM(bl...  35.5 us

profile of v8, /device:TPU:25, one launch (start us, length us, event | category | flops | bytes accessed | tf_op | source)
XLA Modules:
  0.0 36.9 jit_solution(11671670217938547017)
XLA Ops:
  0.6 35.5 %wave_steps.1 = (f32[8,8,128]{2,1,0:T(8,128)S(1)}, f32[8,8,128]{2,1,0:T(8,128)S(1)}, f32[8,8,128]{2,1,0:T(8,128)S(1)}, f32[8,8,128]{2,1,0:T(8,128)S(1)}) custom-call(f32[8,8,128]{2,1,0:T(8,128)} %refs_0_.1, f32[8,8,128]{2,1,0:T(8,128)} %refs_1_.1, f32[8,8,128]{2,1,0:T(8,128)} %refs_2_.1, f32[8,8,128]{2,1,0:T(8,128)} %refs_3_.1, f32[8,8,128]{2,1,0:T(8,128)} %refs_4_.1, ...), custom_call_target="tpu_custom_call" | custom-call | tf_op jit(solution)/shard_map/wave_steps/pallas_call | solution.py:929
  36.2 0.7 %hand_over.1 = (f32[8,8,128]{2,1,0:T(8,128)}, f32[8,8,128]{2,1,0:T(8,128)}, f32[8,8,128]{2,1,0:T(8,128)}, f32[8,8,128]{2,1,0:T(8,128)}) custom-call(f32[8,8,128]{2,1,0:T(8,128)S(1)} %get-tuple-element.8.refs_0_, f32[8,8,128]{2,1,0:T(8,128)S(1)} %get-tuple-element.9.refs_1_, f32[8,8,128]{2,1,0:T(8,128)S(1)} %get-tuple-element.10.refs_2_, ...), custom_call_target="tpu_custom_call" | custom-call | tf_op jit(solution)/shard_map/hand_over/pallas_call | solution.py:987
